TPU v7x, 512 devices: a whole 4x4x16 slice. The times are simulated.
512 devices in a mesh: lat: 8 (over y_lo, x), lon: 64 (over z, y_hi, core).
Axes of the slice: x: 4, y: 4 (y_hi: 2, y_lo: 2; y = y_hi * 2 + y_lo), z: 16, core: 2. Of those that a mesh axis runs over, the one named last changes fastest.
Arguments:
- field_state: bfloat16 [4, 64, 163840], P(None, 'lat', 'lon'), may hold values from -6 to 6
- reservoir_state: bfloat16 [16, 1024, 4, 1024], P('lat', 'lon'), may hold values from -0.8984375 to 0.8984375
- coupling_blocks: bfloat16 [16, 2048, 128], P('lat'), may hold values from -0.375 to 0.375
- coupling_index: int32 [16, 8, 2], P('lat'), may hold values from 0 to 7, as said below
- input_blocks: bfloat16 [16, 1024, 128], P('lat'), may hold values from -0.5 to 0.5
- input_index: int32 [16, 8], P('lat'), may hold values from 0 to 19
- zonal_band_output_matrices: bfloat16 [8, 640, 1024], P('lat'), may hold values from -0.1875 to 0.1875
- region_band: int32 [16], P('lat'), may hold values from 0 to 1
Outputs:
- field_out: bfloat16 [4, 64, 163840], P(None, 'lat', 'lon')
- states_out: bfloat16 [16, 1024, 4, 1024], P('lat', 'lon')
Inputs may be any that keep to these rules, and one draw needn't show every extreme that they name: `coupling_index`: the 2 block columns of one block-row differ. `region_band`: a band of the region row's own latitude group of 2 region rows.
All inputs are finite; a program needn't handle non-finite values.
Results may differ from a plain program's by a relative error of at most 0.0095.
Values may be sent and summed in bfloat16 or wider, within the bound.
A program may use at most 64 MiB of HBM per device.

v0:
```python
import jax
import jax.numpy as jnp
from jax import lax
from jax.sharding import PartitionSpec as P

VARS = 40
STEPS = 3


def extended(cells, sides, width, closed):
    for axis, dim in sides:
        count = lax.axis_size(axis)
        ends = count if closed else count - 1
        head = lax.slice_in_dim(cells, 0, width, axis=dim)
        tail = lax.slice_in_dim(cells, cells.shape[dim] - width, cells.shape[dim], axis=dim)
        cells = jnp.concatenate(
            [
                lax.ppermute(tail, axis, [(i, (i + 1) % count) for i in range(ends)]),
                cells,
                lax.ppermute(head, axis, [((i + 1) % count, i) for i in range(ends)]),
            ],
            axis=dim,
        )
    return cells


def region_inputs(band_slab, region_count, vertical_quantity_total):
    perturbation_copies = band_slab.shape[0]
    pieces = band_slab.reshape(
        perturbation_copies, 8, region_count + 1, 4 * vertical_quantity_total
    )
    windows = jnp.concatenate([pieces[:, :, :-1], pieces[:, :, 1:]], axis=3)
    return windows.transpose(2, 0, 1, 3).reshape(
        region_count * perturbation_copies, 64 * vertical_quantity_total
    )


def reservoir_update(state_rows, input_rows, coupling, coupling_idx, driving, driving_idx):
    row_count = state_rows.shape[0]
    block_rows = coupling_idx.shape[0]
    slot_count = coupling_idx.shape[1]
    block_size = coupling.shape[-1]
    picked = jnp.take(state_rows.reshape(row_count, block_rows, block_size), coupling_idx, axis=1)
    blocks = coupling.reshape(block_rows, slot_count, block_size, block_size)
    recurrent = jnp.einsum("nbki,bkoi->nbo", picked, blocks, preferred_element_type=jnp.float32)
    chosen = jnp.take(input_rows.reshape(row_count, -1, block_size), driving_idx, axis=1)
    drive_blocks = driving.reshape(block_rows, block_size, block_size)
    drive_term = jnp.einsum(
        "nbi,boi->nbo", chosen, drive_blocks, preferred_element_type=jnp.float32
    )
    refreshed_activation = jnp.tanh(recurrent + drive_term)
    return refreshed_activation.reshape(row_count, block_rows * block_size).astype(jnp.bfloat16)


def per_device(
    field_state,
    reservoir_state,
    coupling_blocks,
    coupling_index,
    input_blocks,
    input_index,
    zonal_band_output_matrices,
    region_band,
):
    vertical_quantity_total = VARS
    perturbation_copies, lat_cells, flat_cols = field_state.shape
    meridional_sector_total = flat_cols // (4 * vertical_quantity_total)
    latitude_region_count = lat_cells // 4
    unit_count = reservoir_state.shape[-1]
    readout_local = zonal_band_output_matrices[0]
    current = field_state
    states_now = reservoir_state
    for step_index in range(STEPS):
        padded = extended(current, (("lat", 1),), 2, False)
        padded = extended(padded, (("lon", 2),), 2 * vertical_quantity_total, True)
        updated_rows = []
        for region_row in range(latitude_region_count):
            band_index = region_band[region_row]
            coupling = lax.dynamic_index_in_dim(coupling_blocks, band_index, 0, keepdims=False)
            coupling_idx = lax.dynamic_index_in_dim(coupling_index, band_index, 0, keepdims=False)
            driving = lax.dynamic_index_in_dim(input_blocks, band_index, 0, keepdims=False)
            driving_idx = lax.dynamic_index_in_dim(input_index, band_index, 0, keepdims=False)
            previous = states_now[region_row].reshape(
                meridional_sector_total * perturbation_copies, unit_count
            )
            inputs_now = region_inputs(
                padded[:, 4 * region_row : 4 * region_row + 8],
                meridional_sector_total,
                vertical_quantity_total,
            )
            updated_rows.append(
                reservoir_update(previous, inputs_now, coupling, coupling_idx, driving, driving_idx)
            )
        refreshed_activation = jnp.concatenate(updated_rows, axis=0)
        prediction_sequence = lax.dot_general(
            refreshed_activation,
            readout_local,
            (((1,), (1,)), ((), ())),
            preferred_element_type=jnp.float32,
        )
        prediction_sequence = prediction_sequence.astype(jnp.bfloat16)
        current = (
            prediction_sequence.reshape(
                latitude_region_count,
                meridional_sector_total,
                perturbation_copies,
                4,
                4 * vertical_quantity_total,
            )
            .transpose(2, 0, 3, 1, 4)
            .reshape(
                perturbation_copies,
                4 * latitude_region_count,
                meridional_sector_total * 4 * vertical_quantity_total,
            )
        )
        states_now = refreshed_activation.reshape(
            latitude_region_count, meridional_sector_total, perturbation_copies, unit_count
        )
    return (current, states_now)


def solution(mesh):
    return jax.shard_map(
        per_device,
        mesh=mesh,
        in_specs=(
            P(None, "lat", "lon"),
            P("lat", "lon", None, None),
            P("lat", None, None),
            P("lat", None, None),
            P("lat", None, None),
            P("lat", None),
            P("lat", None, None),
            P("lat"),
        ),
        out_specs=(P(None, "lat", "lon"), P("lat", "lon", None, None)),
        check_vma=False,
    )
```

profile of v0, /device:TPU:6, one launch (start us, length us, event | category | flops | bytes accessed | tf_op | source)
XLA Modules:
  0.0 146.4 jit_solution(5826031233777272130)
XLA Ops:
  0.6 1.8 %fusion.116 = (bf16[4,2,2560]{2,1,0:T(2,128)(2,1)}, bf16[4,2,2560]{2,1,0:T(2,128)(2,1)S(1)}) fusion(bf16[4,8,2560]{2,1,0:T(8,128)(2,1)} %param.12), kind=kLoop, calls=%fused_computation.171 | loop fusion | bytes 163840 | tf_op jit(solution)/shard_map/slice | solution.py:15
  2.4 3.4 %collective-permute-start = (bf16[4,2,2560]{2,1,0:T(2,128)(2,1)}, bf16[4,2,2560]{2,1,0:T(2,128)(2,1)S(1)}, u32[]{:S(2)}, u32[]{:S(2)}) collective-permute-start(bf16[4,2,2560]{2,1,0:T(2,128)(2,1)} %get-tuple-element.46), channel_id=1, source_target_pairs={{0,64},{64,128},{128,192},{192,256},{256,320},{320,384},{384,448},... | collective-permute-start | bytes 122888 | tf_op jit(solution)/shard_map/ppermute | solution.py:18
  5.8 2.4 %collective-permute-start.1 = (bf16[4,2,2560]{2,1,0:T(2,128)(2,1)S(1)}, bf16[4,2,2560]{2,1,0:T(2,128)(2,1)}, u32[]{:S(2)}, u32[]{:S(2)}) collective-permute-start(bf16[4,2,2560]{2,1,0:T(2,128)(2,1)S(1)} %get-tuple-element.47), channel_id=1, source_target_pairs={{64,0},{128,64},{192,128},{256,192},{320,256},{384,320},{448,384},... | collective-permute-start | bytes 122888 | tf_op jit(solution)/shard_map/ppermute | solution.py:20
  8.3 1.3 fusion.117
  13.2 1.4 compare_and_fusion.1
  17.0 1.3 constant_dynamic-slice_fusion.3
  23.1 12.9 %collective-permute-start.3 = (bf16[4,12,80]{2,1,0:T(8,128)(2,1)S(1)}, bf16[4,12,80]{2,1,0:T(8,128)(2,1)S(1)}, u32[]{:S(2)}, u32[]{:S(2)}) collective-permute-start(bf16[4,12,80]{2,1,0:T(8,128)(2,1)S(1)} %get-tuple-element.38), channel_id=1, source_target_pairs={{1,0},{2,1},{3,2},{4,3},{5,4},{6,5},{7,6},{8,7},{9,8},{10,9},{11,1... | collective-permute-start | bytes 23048 | tf_op jit(solution)/shard_map/ppermute | solution.py:20
  36.0 1.9 %collective-permute-start.2 = (bf16[4,12,80]{2,1,0:T(8,128)(2,1)S(1)}, bf16[4,12,80]{2,1,0:T(8,128)(2,1)S(1)}, u32[]{:S(2)}, u32[]{:S(2)}) collective-permute-start(bf16[4,12,80]{2,1,0:T(8,128)(2,1)S(1)} %get-tuple-element.39), channel_id=1, source_target_pairs={{0,1},{1,2},{2,3},{3,4},{4,5},{5,6},{6,7},{7,8},{8,9},{9,10},{10,1... | collective-permute-start | bytes 23048 | tf_op jit(solution)/shard_map/ppermute | solution.py:18
  38.0 6.7 %collective-permute-done.2 = bf16[4,12,80]{2,1,0:T(8,128)(2,1)S(1)} collective-permute-done((bf16[4,12,80]{2,1,0:T(8,128)(2,1)S(1)}, bf16[4,12,80]{2,1,0:T(8,128)(2,1)S(1)}, u32[]{:S(2)}, u32[]{:S(2)}) %collective-permute-start.2) | collective-permute-done | bytes 7712 | tf_op jit(solution)/shard_map/ppermute | solution.py:18
  44.7 1.1 concatenate.46
  45.8 1.8 %fusion.109 = (bf16[4,8,2720]{2,1,0:T(8,128)(2,1)}, bf16[4,8,2720]{2,1,0:T(8,128)(2,1)}) fusion(bf16[4,12,2720]{2,1,0:T(8,128)(2,1)} %concatenate.46), kind=kLoop, calls=%fused_computation.164 | loop fusion | bytes 696320 | tf_op jit(solution)/shard_map/slice | solution.py:87
  47.6 1.3 reshape.104
  49.3 1.2 reshape_reshape.19
  50.5 1.8 %copy.71 = bf16[64,20,128]{2,0,1:T(8,128)(2,1)} copy(bf16[64,20,128]{2,1,0:T(8,128)(2,1)} %reshape_reshape.19) | data formatting | bytes 655360 | tf_op jit(solution)/shard_map/reshape;reshape | solution.py:46
  52.3 1.3 reshape.101
  54.0 1.2 reshape_reshape.18
  55.2 1.8 %copy.64 = bf16[64,20,128]{2,0,1:T(8,128)(2,1)} copy(bf16[64,20,128]{2,1,0:T(8,128)(2,1)} %reshape_reshape.18) | data formatting | bytes 655360 | tf_op jit(solution)/shard_map/reshape;reshape | solution.py:46
  57.0 1.7 %gather_fusion.4 = bf16[8,64,128]{2,1,0:T(8,128)(2,1)S(1)} fusion(bf16[64,20,128]{2,0,1:T(8,128)(2,1)} %copy.71, s32[1024]{0:T(1024)} %get-tuple-element.54), kind=kCustom, calls=%fused_computation.7.clone | custom fusion | bytes 262176 | tf_op jit(solution)/shard_map/jit(_take)/gather | solution.py:46
  58.7 1.3 fusion.22
  60.6 1.7 %gather_fusion.1 = bf16[8,64,128]{2,1,0:T(8,128)(2,1)S(1)} fusion(bf16[64,20,128]{2,0,1:T(8,128)(2,1)} %copy.64, s32[1024]{0:T(1024)} %get-tuple-element.56), kind=kCustom, calls=%fused_computation.1.clone | custom fusion | bytes 262176 | tf_op jit(solution)/shard_map/jit(_take)/gather | solution.py:46
  63.3 2.1 %fusion.12 = bf16[128,640]{1,0:T(8,128)(2,1)} fusion(bf16[1,640,1024]{2,1,0:T(8,128)(2,1)S(1)} %copy-done, bf16[64,1024]{1,0:T(8,128)(2,1)} %copy_bitcast_fusion.4, bf16[64,1024]{1,0:T(8,128)(2,1)S(1)} %copy_bitcast_fusion.5), kind=kOutput, calls=%fused_computation.36 | convolution fusion | flops 168378368 | bytes 1736704 | tf_op jit(solution)/shard_map/dot_general | solution.py:95
  65.4 1.1 reshape.105
  67.3 1.3 reshape.106
  69.3 4.7 %collective-permute-start.4 = (bf16[4,2,2560]{2,1,0:T(2,128)(2,1)}, bf16[4,2,2560]{2,1,0:T(2,128)(2,1)S(1)}, u32[]{:S(2)}, u32[]{:S(2)}) collective-permute-start(bf16[4,2,2560]{2,1,0:T(2,128)(2,1)} %get-tuple-element.44), channel_id=1, source_target_pairs={{0,64},{64,128},{128,192},{192,256},{256,320},{320,384},{384,448},... | collective-permute-start | bytes 122888 | tf_op jit(solution)/shard_map/ppermute | solution.py:18
  74.0 1.9 %collective-permute-start.5 = (bf16[4,2,2560]{2,1,0:T(2,128)(2,1)}, bf16[4,2,2560]{2,1,0:T(2,128)(2,1)}, u32[]{:S(2)}, u32[]{:S(2)}) collective-permute-start(bf16[4,2,2560]{2,1,0:T(2,128)(2,1)} %get-tuple-element.45), channel_id=1, source_target_pairs={{64,0},{128,64},{192,128},{256,192},{320,256},{384,320},{448,384},... | collective-permute-start | bytes 122888 | tf_op jit(solution)/shard_map/ppermute | solution.py:20
  78.2 4.1 %collective-permute-done.5 = bf16[4,2,2560]{2,1,0:T(2,128)(2,1)} collective-permute-done((bf16[4,2,2560]{2,1,0:T(2,128)(2,1)}, bf16[4,2,2560]{2,1,0:T(2,128)(2,1)}, u32[]{:S(2)}, u32[]{:S(2)}) %collective-permute-start.5) | collective-permute-done | bytes 40992 | tf_op jit(solution)/shard_map/ppermute | solution.py:20
  82.3 1.1 pad_maximum_fusion.1
  83.5 1.9 %collective-permute-start.7 = (bf16[4,12,80]{2,1,0:T(8,128)(2,1)S(1)}, bf16[4,12,80]{2,1,0:T(8,128)(2,1)S(1)}, u32[]{:S(2)}, u32[]{:S(2)}) collective-permute-start(bf16[4,12,80]{2,1,0:T(8,128)(2,1)S(1)} %get-tuple-element.36), channel_id=1, source_target_pairs={{1,0},{2,1},{3,2},{4,3},{5,4},{6,5},{7,6},{8,7},{9,8},{10,9},{11,1... | collective-permute-start | bytes 23048 | tf_op jit(solution)/shard_map/ppermute | solution.py:20
  85.4 2.4 %collective-permute-start.6 = (bf16[4,12,80]{2,1,0:T(8,128)(2,1)S(1)}, bf16[4,12,80]{2,1,0:T(8,128)(2,1)S(1)}, u32[]{:S(2)}, u32[]{:S(2)}) collective-permute-start(bf16[4,12,80]{2,1,0:T(8,128)(2,1)S(1)} %get-tuple-element.37), channel_id=1, source_target_pairs={{0,1},{1,2},{2,3},{3,4},{4,5},{5,6},{6,7},{7,8},{8,9},{9,10},{10,1... | collective-permute-start | bytes 23048 | tf_op jit(solution)/shard_map/ppermute | solution.py:18
  88.9 5.2 %collective-permute-done.6 = bf16[4,12,80]{2,1,0:T(8,128)(2,1)S(1)} collective-permute-done((bf16[4,12,80]{2,1,0:T(8,128)(2,1)S(1)}, bf16[4,12,80]{2,1,0:T(8,128)(2,1)S(1)}, u32[]{:S(2)}, u32[]{:S(2)}) %collective-permute-start.6) | collective-permute-done | bytes 7712 | tf_op jit(solution)/shard_map/ppermute | solution.py:18
  94.1 1.1 concatenate.51
  95.2 1.8 %fusion.108 = (bf16[4,8,2720]{2,1,0:T(8,128)(2,1)S(1)}, bf16[4,8,2720]{2,1,0:T(8,128)(2,1)}) fusion(bf16[4,12,2720]{2,1,0:T(8,128)(2,1)} %concatenate.51), kind=kLoop, calls=%fused_computation.163 | loop fusion | bytes 696320 | tf_op jit(solution)/shard_map/slice | solution.py:87
  97.7 1.2 reshape_reshape.21
  100.0 1.3 gather_fusion.8
  101.3 1.2 fusion.24
  103.8 1.3 reshape.107
  105.5 1.2 reshape_reshape.20
  107.8 1.3 gather_fusion.5
  109.2 1.3 fusion.23
  110.5 2.1 %fusion.15 = bf16[128,640]{1,0:T(8,128)(2,1)} fusion(bf16[1,640,1024]{2,1,0:T(8,128)(2,1)S(1)} %copy-done, bf16[64,1024]{1,0:T(8,128)(2,1)} %copy_bitcast_fusion.2, bf16[64,1024]{1,0:T(8,128)(2,1)S(1)} %copy_bitcast_fusion.3), kind=kOutput, calls=%fused_computation.37 | convolution fusion | flops 168378368 | bytes 1736704 | tf_op jit(solution)/shard_map/dot_general | solution.py:95
  112.7 1.1 reshape.109
  114.6 1.3 reshape.110
  116.6 1.9 %collective-permute-start.8 = (bf16[4,2,2560]{2,1,0:T(2,128)(2,1)}, bf16[4,2,2560]{2,1,0:T(2,128)(2,1)}, u32[]{:S(2)}, u32[]{:S(2)}) collective-permute-start(bf16[4,2,2560]{2,1,0:T(2,128)(2,1)} %get-tuple-element.42), channel_id=1, source_target_pairs={{0,64},{64,128},{128,192},{192,256},{256,320},{320,384},{384,448},... | collective-permute-start | bytes 122888 | tf_op jit(solution)/shard_map/ppermute | solution.py:18
  118.5 4.1 %collective-permute-start.9 = (bf16[4,2,2560]{2,1,0:T(2,128)(2,1)}, bf16[4,2,2560]{2,1,0:T(2,128)(2,1)}, u32[]{:S(2)}, u32[]{:S(2)}) collective-permute-start(bf16[4,2,2560]{2,1,0:T(2,128)(2,1)} %get-tuple-element.43), channel_id=1, source_target_pairs={{64,0},{128,64},{192,128},{256,192},{320,256},{384,320},{448,384},... | collective-permute-start | bytes 122888 | tf_op jit(solution)/shard_map/ppermute | solution.py:20
  124.3 2.5 %collective-permute-done.9 = bf16[4,2,2560]{2,1,0:T(2,128)(2,1)} collective-permute-done((bf16[4,2,2560]{2,1,0:T(2,128)(2,1)}, bf16[4,2,2560]{2,1,0:T(2,128)(2,1)}, u32[]{:S(2)}, u32[]{:S(2)}) %collective-permute-start.9) | collective-permute-done | bytes 40992 | tf_op jit(solution)/shard_map/ppermute | solution.py:20
  128.0 1.9 %collective-permute-start.11 = (bf16[4,12,80]{2,1,0:T(8,128)(2,1)S(1)}, bf16[4,12,80]{2,1,0:T(8,128)(2,1)S(1)}, u32[]{:S(2)}, u32[]{:S(2)}) collective-permute-start(bf16[4,12,80]{2,1,0:T(8,128)(2,1)S(1)} %get-tuple-element.34), channel_id=1, source_target_pairs={{1,0},{2,1},{3,2},{4,3},{5,4},{6,5},{7,6},{8,7},{9,8},{10,9},{11,1... | collective-permute-start | bytes 23048 | tf_op jit(solution)/shard_map/ppermute | solution.py:20
  129.9 2.4 %collective-permute-start.10 = (bf16[4,12,80]{2,1,0:T(8,128)(2,1)S(1)}, bf16[4,12,80]{2,1,0:T(8,128)(2,1)S(1)}, u32[]{:S(2)}, u32[]{:S(2)}) collective-permute-start(bf16[4,12,80]{2,1,0:T(8,128)(2,1)S(1)} %get-tuple-element.35), channel_id=1, source_target_pairs={{0,1},{1,2},{2,3},{3,4},{4,5},{5,6},{6,7},{7,8},{8,9},{9,10},{10,1... | collective-permute-start | bytes 23048 | tf_op jit(solution)/shard_map/ppermute | solution.py:18
  132.7 5.9 %collective-permute-done.10 = bf16[4,12,80]{2,1,0:T(8,128)(2,1)S(1)} collective-permute-done((bf16[4,12,80]{2,1,0:T(8,128)(2,1)S(1)}, bf16[4,12,80]{2,1,0:T(8,128)(2,1)S(1)}, u32[]{:S(2)}, u32[]{:S(2)}) %collective-permute-start.10) | collective-permute-done | bytes 7712 | tf_op jit(solution)/shard_map/ppermute | solution.py:18
  (106 shorter events, 31.2 us)
Async XLA Ops:
  0.6 62.7 %copy-start = (bf16[1,640,1024]{2,1,0:T(8,128)(2,1)S(1)}, bf16[1,640,1024]{2,1,0:T(8,128)(2,1)}, u32[]{:S(2)}) copy-start(bf16[1,640,1024]{2,1,0:T(8,128)(2,1)} %param.18) | copy-start | bytes 3932164
  2.4 19.7 %collective-permute-start = (bf16[4,2,2560]{2,1,0:T(2,128)(2,1)}, bf16[4,2,2560]{2,1,0:T(2,128)(2,1)S(1)}, u32[]{:S(2)}, u32[]{:S(2)}) collective-permute-start(bf16[4,2,2560]{2,1,0:T(2,128)(2,1)} %get-tuple-element.46), channel_id=1, source_target_pairs={{0,64},{64,128},{128,192},{192,256},{256,320},{320,384},{384,448},... | collective-permute-start | bytes 122888 | tf_op jit(solution)/shard_map/ppermute | solution.py:18
  5.8 16.3 %collective-permute-start.1 = (bf16[4,2,2560]{2,1,0:T(2,128)(2,1)S(1)}, bf16[4,2,2560]{2,1,0:T(2,128)(2,1)}, u32[]{:S(2)}, u32[]{:S(2)}) collective-permute-start(bf16[4,2,2560]{2,1,0:T(2,128)(2,1)S(1)} %get-tuple-element.47), channel_id=1, source_target_pairs={{64,0},{128,64},{192,128},{256,192},{320,256},{384,320},{448,384},... | collective-permute-start | bytes 122888 | tf_op jit(solution)/shard_map/ppermute | solution.py:20
  20.7 1.4 copy-start.6
  20.7 17.3 %copy-start.5 = (bf16[2,1024,128]{2,1,0:T(8,128)(2,1)S(1)}, bf16[2,1024,128]{2,1,0:T(8,128)(2,1)}, u32[]{:S(2)}) copy-start(bf16[2,1024,128]{2,1,0:T(8,128)(2,1)} %param.16) | copy-start | bytes 1572868
  23.1 14.9 %collective-permute-start.3 = (bf16[4,12,80]{2,1,0:T(8,128)(2,1)S(1)}, bf16[4,12,80]{2,1,0:T(8,128)(2,1)S(1)}, u32[]{:S(2)}, u32[]{:S(2)}) collective-permute-start(bf16[4,12,80]{2,1,0:T(8,128)(2,1)S(1)} %get-tuple-element.38), channel_id=1, source_target_pairs={{1,0},{2,1},{3,2},{4,3},{5,4},{6,5},{7,6},{8,7},{9,8},{10,9},{11,1... | collective-permute-start | bytes 23048 | tf_op jit(solution)/shard_map/ppermute | solution.py:20
  36.0 8.7 %collective-permute-start.2 = (bf16[4,12,80]{2,1,0:T(8,128)(2,1)S(1)}, bf16[4,12,80]{2,1,0:T(8,128)(2,1)S(1)}, u32[]{:S(2)}, u32[]{:S(2)}) collective-permute-start(bf16[4,12,80]{2,1,0:T(8,128)(2,1)S(1)} %get-tuple-element.39), channel_id=1, source_target_pairs={{0,1},{1,2},{2,3},{3,4},{4,5},{5,6},{6,7},{7,8},{8,9},{9,10},{10,1... | collective-permute-start | bytes 23048 | tf_op jit(solution)/shard_map/ppermute | solution.py:18
  68.6 7.3 %copy-start.4 = (bf16[4,8,2560]{2,1,0:T(8,128)(2,1)}, bf16[4,8,2560]{2,1,0:T(8,128)(2,1)S(1)}, u32[]{:S(2)}) copy-start(bf16[4,8,2560]{2,1,0:T(8,128)(2,1)S(1)} %reshape.106) | copy-start | bytes 491524
  69.3 8.9 %collective-permute-start.4 = (bf16[4,2,2560]{2,1,0:T(2,128)(2,1)}, bf16[4,2,2560]{2,1,0:T(2,128)(2,1)S(1)}, u32[]{:S(2)}, u32[]{:S(2)}) collective-permute-start(bf16[4,2,2560]{2,1,0:T(2,128)(2,1)} %get-tuple-element.44), channel_id=1, source_target_pairs={{0,64},{64,128},{128,192},{192,256},{256,320},{320,384},{384,448},... | collective-permute-start | bytes 122888 | tf_op jit(solution)/shard_map/ppermute | solution.py:18
  74.0 8.3 %collective-permute-start.5 = (bf16[4,2,2560]{2,1,0:T(2,128)(2,1)}, bf16[4,2,2560]{2,1,0:T(2,128)(2,1)}, u32[]{:S(2)}, u32[]{:S(2)}) collective-permute-start(bf16[4,2,2560]{2,1,0:T(2,128)(2,1)} %get-tuple-element.45), channel_id=1, source_target_pairs={{64,0},{128,64},{192,128},{256,192},{320,256},{384,320},{448,384},... | collective-permute-start | bytes 122888 | tf_op jit(solution)/shard_map/ppermute | solution.py:20
  83.5 5.4 %collective-permute-start.7 = (bf16[4,12,80]{2,1,0:T(8,128)(2,1)S(1)}, bf16[4,12,80]{2,1,0:T(8,128)(2,1)S(1)}, u32[]{:S(2)}, u32[]{:S(2)}) collective-permute-start(bf16[4,12,80]{2,1,0:T(8,128)(2,1)S(1)} %get-tuple-element.36), channel_id=1, source_target_pairs={{1,0},{2,1},{3,2},{4,3},{5,4},{6,5},{7,6},{8,7},{9,8},{10,9},{11,1... | collective-permute-start | bytes 23048 | tf_op jit(solution)/shard_map/ppermute | solution.py:20
  85.4 8.7 %collective-permute-start.6 = (bf16[4,12,80]{2,1,0:T(8,128)(2,1)S(1)}, bf16[4,12,80]{2,1,0:T(8,128)(2,1)S(1)}, u32[]{:S(2)}, u32[]{:S(2)}) collective-permute-start(bf16[4,12,80]{2,1,0:T(8,128)(2,1)S(1)} %get-tuple-element.37), channel_id=1, source_target_pairs={{0,1},{1,2},{2,3},{3,4},{4,5},{5,6},{6,7},{7,8},{8,9},{9,10},{10,1... | collective-permute-start | bytes 23048 | tf_op jit(solution)/shard_map/ppermute | solution.py:18
  97.6 3.8 %copy-start.2 = (f32[8,128,64]{1,2,0:T(8,128)S(1)}, f32[8,128,64]{1,2,0:T(8,128)}, u32[]{:S(2)}) copy-start(f32[8,128,64]{1,2,0:T(8,128)} %convolution_bitcast_fusion.1) | copy-start | bytes 786436
  105.4 3.8 %copy-start.8 = (pred[8]{0:T(512)(128)(4,1)S(1)}, pred[8]{0:T(512)(128)(4,1)}, u32[]{:S(2)}) copy-start(pred[8]{0:T(512)(128)(4,1)} %get-tuple-element.50) | copy-start | bytes 28
  115.9 7.8 %copy-start.3 = (bf16[4,8,2560]{2,1,0:T(8,128)(2,1)}, bf16[4,8,2560]{2,1,0:T(8,128)(2,1)S(1)}, u32[]{:S(2)}) copy-start(bf16[4,8,2560]{2,1,0:T(8,128)(2,1)S(1)} %reshape.110) | copy-start | bytes 491524
  116.6 7.7 %collective-permute-start.8 = (bf16[4,2,2560]{2,1,0:T(2,128)(2,1)}, bf16[4,2,2560]{2,1,0:T(2,128)(2,1)}, u32[]{:S(2)}, u32[]{:S(2)}) collective-permute-start(bf16[4,2,2560]{2,1,0:T(2,128)(2,1)} %get-tuple-element.42), channel_id=1, source_target_pairs={{0,64},{64,128},{128,192},{192,256},{256,320},{320,384},{384,448},... | collective-permute-start | bytes 122888 | tf_op jit(solution)/shard_map/ppermute | solution.py:18
  118.5 8.3 %collective-permute-start.9 = (bf16[4,2,2560]{2,1,0:T(2,128)(2,1)}, bf16[4,2,2560]{2,1,0:T(2,128)(2,1)}, u32[]{:S(2)}, u32[]{:S(2)}) collective-permute-start(bf16[4,2,2560]{2,1,0:T(2,128)(2,1)} %get-tuple-element.43), channel_id=1, source_target_pairs={{64,0},{128,64},{192,128},{256,192},{320,256},{384,320},{448,384},... | collective-permute-start | bytes 122888 | tf_op jit(solution)/shard_map/ppermute | solution.py:20
  128.0 4.7 %collective-permute-start.11 = (bf16[4,12,80]{2,1,0:T(8,128)(2,1)S(1)}, bf16[4,12,80]{2,1,0:T(8,128)(2,1)S(1)}, u32[]{:S(2)}, u32[]{:S(2)}) collective-permute-start(bf16[4,12,80]{2,1,0:T(8,128)(2,1)S(1)} %get-tuple-element.34), channel_id=1, source_target_pairs={{1,0},{2,1},{3,2},{4,3},{5,4},{6,5},{7,6},{8,7},{9,8},{10,9},{11,1... | collective-permute-start | bytes 23048 | tf_op jit(solution)/shard_map/ppermute | solution.py:20
  129.9 8.7 %collective-permute-start.10 = (bf16[4,12,80]{2,1,0:T(8,128)(2,1)S(1)}, bf16[4,12,80]{2,1,0:T(8,128)(2,1)S(1)}, u32[]{:S(2)}, u32[]{:S(2)}) collective-permute-start(bf16[4,12,80]{2,1,0:T(8,128)(2,1)S(1)} %get-tuple-element.35), channel_id=1, source_target_pairs={{0,1},{1,2},{2,3},{3,4},{4,5},{5,6},{6,7},{7,8},{8,9},{9,10},{10,1... | collective-permute-start | bytes 23048 | tf_op jit(solution)/shard_map/ppermute | solution.py:18
  141.7 1.7 %copy-start.1 = (f32[8,128,64]{1,2,0:T(8,128)S(1)}, f32[8,128,64]{1,2,0:T(8,128)}, u32[]{:S(2)}) copy-start(f32[8,128,64]{1,2,0:T(8,128)} %convolution_bitcast_fusion) | copy-start | bytes 786436
  141.7 1.7 %copy-start.7 = (pred[8]{0:T(512)(128)(4,1)S(1)}, pred[8]{0:T(512)(128)(4,1)}, u32[]{:S(2)}) copy-start(pred[8]{0:T(512)(128)(4,1)} %get-tuple-element.4) | copy-start | bytes 28
where the time goes:
time: 148 us; the launch traced here: 146 us
  local copies, waits for them, and re-layouts  52.8 us (36%)
  starting transfers between devices  41.9 us (28%)
  waiting for transfers between devices  24.5 us (17%)
  matrix products  15.1 us (10%)
  other arithmetic  7.27 us (5%)
  between operations  4.91 us (3%)
    ppermute x6, starting transfers between devices, extended(): lax.ppermute(head, axis, [((i + 1) % count, i) for i in range(ends)])  25.2 us
    ppermute x6, waiting for transfers between devices, extended(): lax.ppermute(tail, axis, [(i, (i + 1) % count) for i in range(ends)])  17.8 us
    ppermute x6, starting transfers between devices, extended(): lax.ppermute(tail, axis, [(i, (i + 1) % count) for i in range(ends)])  16.7 us
    another operation x12, local copies, waits for them, and re-layouts, reservoir_update(): input_rows.reshape(row_count, -1, block_size)  11.8 us
    gather x6, local copies, waits for them, and re-layouts, reservoir_update(): jnp.take(input_rows.reshape(row_count, -1, block_size), driving_idx, axis=1)  7.41 us
    ppermute x6, waiting for transfers between devices, extended(): lax.ppermute(head, axis, [((i + 1) % count, i) for i in range(ends)])  6.67 us
    dot_general x6, matrix products, reservoir_update(): jnp.einsum('nbi,boi->nbo', chosen, drive_blocks, preferred_element_type=j...  5.44 us
    reshape x6, local copies, waits for them, and re-layouts, region_inputs(): band_slab.reshape(perturbation_copies, 8, region_count + 1, 4 * vertical_...  4.96 us
  transfers between devices with their start and end apart: 12, of which 5 were waited for; matrix products, arithmetic and copies ran while one was open for 11% of the time, Pallas kernels for 0%

commit v1 on v0

v1 whole, which is shorter than its diff:
```python
import functools

import jax
import jax.numpy as jnp
from jax import lax
from jax.experimental import pallas as pl
from jax.experimental.pallas import tpu as pltpu
from jax.sharding import PartitionSpec as P

MESH = pl.DeviceIdType.MESH
STEPS = 3
F32 = jnp.float32
BF16 = jnp.bfloat16

DIRS = ((-1, 0), (1, 0), (0, -1), (0, 1), (-1, -1), (-1, 1), (1, -1), (1, 1))


def dot_nt(x, w):
    return lax.dot_general(x, w, (((1,), (1,)), ((), ())), preferred_element_type=F32)


def lanes(rows):
    return lax.broadcasted_iota(jnp.int32, (rows, 128), 1)


def roll(x, by):
    return pltpu.roll(x, by, 1)


def minus_parts(r0, r1, r2):
    lane = lanes(r0.shape[0])
    b0 = jnp.where(lane < 48, roll(r0, 48), roll(r1, 48))
    r2r = roll(r2, 80)
    b2 = jnp.where(lane < 80, roll(r1, 80), r2r)
    return b0, b2, r2r


def plus_parts(r0, r1):
    r0r = roll(r0, 112)
    return r0r, r0r, roll(r1, 16)


def windows(r0, r1, r2, n):
    rows = 8 * n
    lane = lanes(rows)
    m = slice(0, rows)
    c = slice(8, rows + 8)
    p = slice(16, rows + 16)
    m0, m2, m3 = minus_parts(r0[m], r1[m], r2[m])
    p1, p2, p4 = plus_parts(r0[p], r1[p])
    c0 = roll(r0[c], 80)
    c1 = roll(r1[c], 80)
    d1 = roll(r1[c], 112)
    d2 = roll(r2[c], 112)
    b0 = jnp.where(lane < 80, m0, c0)
    b1 = jnp.where(lane < 80, c0, jnp.where(lane < 112, c1, p1))
    b2 = jnp.where(lane < 64, p2, m2)
    b3 = jnp.where(lane < 16, m3, jnp.where(lane < 112, d1, d2))
    b4 = jnp.where(lane < 48, d2, p4)
    return b0, b1, b2, b3, b4


def kernel(
    cidx, qidx, rband,
    field_hbm, state_hbm, coup_hbm, drive_hbm, read_hbm,
    field_out, state_out,
    field_in, state_in, coup, drive, read,
    states, pre, win, raw, halo, edge, edge_in, ta, tb,
    local_sem, send_sem, recv_sem,
):
    lat, lon = lax.axis_index("lat"), lax.axis_index("lon")
    nlat, nlon = lax.axis_size("lat"), lax.axis_size("lon")
    west, east = lax.rem(lon + nlon - 1, nlon), lax.rem(lon + 1, nlon)
    has_south = lat > 0
    has_north = lat < nlat - 1

    def target(d):
        dl, do = DIRS[d]
        return (lat + dl, west if do < 0 else (east if do > 0 else lon))

    def by_side(fn):
        for d in (0, 4, 5, 1, 6, 7, 2, 3):
            dl = DIRS[d][0]
            if dl == 0:
                fn(d)
            else:
                pl.when(has_south if dl < 0 else has_north)(functools.partial(fn, d))

    barrier = pltpu.get_barrier_semaphore()
    by_side(lambda d: pl.semaphore_signal(barrier, inc=1, device_id=target(d), device_id_type=MESH))

    loads = [
        pltpu.make_async_copy(src, dst, local_sem.at[n])
        for n, (src, dst) in enumerate(
            ((field_hbm, field_in), (state_hbm, state_in), (coup_hbm, coup), (drive_hbm, drive), (read_hbm, read))
        )
    ]
    for load in loads:
        load.start()

    @pl.when(lat == 0)
    def _():
        halo[:, 0] = jnp.zeros(halo.shape[:1] + halo.shape[2:], BF16)
        edge_in[:, 6:8] = jnp.zeros((STEPS, 2) + edge_in.shape[2:], BF16)

    @pl.when(lat == nlat - 1)
    def _():
        halo[:, 1] = jnp.zeros(halo.shape[:1] + halo.shape[2:], BF16)
        edge_in[:, 4:6] = jnp.zeros((STEPS, 2) + edge_in.shape[2:], BF16)

    def message(step, d):
        if d == 0:
            src, dst = raw.at[step, 0], halo.at[step, 1]
        elif d == 1:
            src, dst = raw.at[step, 3], halo.at[step, 0]
        else:
            src, dst = edge.at[step, 0 if DIRS[d][1] < 0 else 1], edge_in.at[step, d]
        return pltpu.make_async_remote_copy(
            src_ref=src, dst_ref=dst, send_sem=send_sem.at[step, d], recv_sem=recv_sem.at[step, d],
            device_id=target(d), device_id_type=MESH,
        )

    def wait_recv(step, d):
        dl = DIRS[d][0]
        if dl == 0:
            message(step, d).wait_recv()
        else:
            @pl.when(has_north if dl < 0 else has_south)
            def _():
                message(step, d).wait_recv()

    def put_raw(step, pair, r):
        for k in range(3):
            raw[step, pair, k] = r[k].astype(BF16)

    def put_edges(step, rs):
        for k in range(3):
            first = jnp.concatenate([rs[p][k][0:4] for p in range(4)], axis=0)
            last = jnp.concatenate([rs[p][k][60:64] for p in range(4)], axis=0)
            edge[step, 0, k] = first.astype(BF16)
            edge[step, 1, k] = last.astype(BF16)

    def send(step):
        by_side(lambda d: message(step, d).start())

    loads[0].wait()
    lane8 = lanes(8)
    for m in range(4):
        f = [field_in[m, :, 128 * k:128 * (k + 1)].astype(F32) for k in range(20)]
        for j in range(16):
            q, off = (160 * j) // 128, (160 * j) % 128
            row = (j % 8) * 8 + (j // 8) * 4 + m
            if off == 0:
                w0, w1 = f[q], f[q + 1]
            else:
                w1 = roll(f[q + 1], 128 - off)
                w0 = jnp.where(lane8 < 128 - off, roll(f[q], 128 - off), w1)
            ta[pl.ds(row, 8, stride=64), :] = w0
            tb[pl.ds(row, 8, stride=64), :] = w1
    lane64 = lanes(64)
    rs = []
    for p in range(4):
        a0, a1 = ta[128 * p:128 * p + 64], tb[128 * p:128 * p + 64]
        b0, b1 = roll(ta[128 * p + 64:128 * p + 128], 32), roll(tb[128 * p + 64:128 * p + 128], 32)
        r = (a0, jnp.where(lane64 < 32, a1, b0), jnp.where(lane64 < 32, b0, b1))
        put_raw(0, p, r)
        rs.append(r)
    put_edges(0, rs)

    pl.semaphore_wait(
        barrier, 2 + 3 * has_south.astype(jnp.int32) + 3 * has_north.astype(jnp.int32)
    )
    send(0)

    loads[1].wait()
    for i in range(2):
        for t in range(4):
            tiles = []
            for jl in (2 * t, 2 * t + 1):
                tiles.append(state_in[i, jl].astype(F32))
                tiles.append(state_in[i, jl + 8].astype(F32))
            rows = jnp.concatenate(tiles, axis=0).astype(BF16)
            for c in range(8):
                states[c, 64 * i + 16 * t:64 * i + 16 * t + 16] = rows[:, 128 * c:128 * (c + 1)]
    loads[2].wait()
    loads[3].wait()

    bands = [rband[i] for i in range(2)]

    for step in range(STEPS):
        for i in range(2):
            for b in range(8):
                x = jnp.concatenate(
                    [states[cidx[bands[i], k, b], 64 * i:64 * i + 64] for k in range(2)], axis=1
                )
                w = jnp.concatenate(
                    [coup[bands[i], (2 * b + k) * 128:(2 * b + k + 1) * 128] for k in range(2)], axis=1
                )
                pre[i, b] = dot_nt(x, w)
        for p in range(4):
            ext = []
            for k in range(3):
                r = raw[step, p, k].astype(F32)
                before = jnp.concatenate([r[56:60], r[56:60]], axis=0)
                after = jnp.concatenate([r[4:8], r[4:8]], axis=0)
                ext.append(jnp.concatenate([before, r, after], axis=0))
            for k, block in enumerate(windows(*ext, 8)):
                win[5 + 5 * p + k] = block.astype(BF16)

        for d in range(8):
            wait_recv(step, d)

        lane16 = lanes(16)
        row16 = lax.broadcasted_iota(jnp.int32, (16, 128), 0)
        es = [edge_in[step, 3, k].astype(F32) for k in range(3)]
        ws = minus_parts(*es)
        el = [edge_in[step, 2, k].astype(F32) for k in range(3)]
        wl = plus_parts(el[0], el[1])
        minus_mask = (lane16 < 80, lane16 >= 64, lane16 < 16)
        plus_mask = (lane16 >= 112, lane16 < 64, lane16 >= 48)
        for p in range(4):
            for n, k in enumerate((0, 2, 3)):
                part = ws[n] if p == 0 else pltpu.roll(ws[n], 16 - 4 * p, 0)
                at = 5 + 5 * p + k
                old = win[at, 0:16].astype(F32)
                win[at, 0:16] = jnp.where((row16 < 4) & minus_mask[n], part, old).astype(BF16)
            for n, k in enumerate((1, 2, 4)):
                part = wl[n] if p == 3 else pltpu.roll(wl[n], 12 - 4 * p, 0)
                at = 5 + 5 * p + k
                old = win[at, 48:64].astype(F32)
                win[at, 48:64] = jnp.where((row16 >= 12) & plus_mask[n], part, old).astype(BF16)

        for side, (p, dw, de) in enumerate(((3, 7, 6), (0, 5, 4))):
            ext = []
            for k in range(3):
                r = halo[step, side, k].astype(F32)
                from_west = edge_in[step, dw, k].astype(F32)[4 * p:4 * p + 4]
                from_east = edge_in[step, de, k].astype(F32)[4 * p:4 * p + 4]
                ext.append(jnp.concatenate([from_west, r[56:60], r, r[4:8], from_east], axis=0))
            for k, block in enumerate(windows(*ext, 8)):
                win[25 * side + k] = block.astype(BF16)

        for i in range(2):
            for b in range(8):
                x = win[10 * i + qidx[bands[i], b]]
                w = drive[bands[i], 128 * b:128 * (b + 1)]
                new = jnp.tanh(pre[i, b] + dot_nt(x, w))
                states[b, 64 * i:64 * i + 64] = new.astype(BF16)
                if step == STEPS - 1:
                    for jl in range(8):
                        state_out[i, jl, :, 128 * b:128 * (b + 1)] = new[8 * jl:8 * jl + 4].astype(BF16)
                        state_out[i, jl + 8, :, 128 * b:128 * (b + 1)] = new[8 * jl + 4:8 * jl + 8].astype(BF16)
        if step == 0:
            loads[4].wait()
        x = jnp.concatenate([states[c] for c in range(8)], axis=1)
        if step < STEPS - 1:
            rs = [None] * 4
            for h in range(2):
                y = dot_nt(x, read[0, 320 * h:320 * h + 320])
                y = jnp.concatenate([y, jnp.zeros((128, 64), F32)], axis=1)
                for i in range(2):
                    r = tuple(y[64 * i:64 * i + 64, 128 * k:128 * (k + 1)] for k in range(3))
                    put_raw(step + 1, 2 * i + h, r)
                    rs[2 * i + h] = r
            put_edges(step + 1, rs)
            send(step + 1)
        else:
            for dy in range(4):
                y = dot_nt(x, read[0, 160 * dy:160 * dy + 160])
                for i in range(2):
                    at = 64 * (4 * i + dy)
                    ta[at:at + 64] = y[64 * i:64 * i + 64, 0:128]
                    tb[at:at + 64, 0:32] = y[64 * i:64 * i + 64, 128:160]

    for m in range(4):
        cols = []
        prev = None
        for j in range(16):
            off = (160 * j) % 128
            row = (j % 8) * 8 + (j // 8) * 4 + m
            v0 = ta[pl.ds(row, 8, stride=64), :]
            v1 = tb[pl.ds(row, 8, stride=64), :]
            if off == 0:
                cols.append(v0)
                prev = (v0, v1, 0)
                continue
            r0, r1 = roll(v0, off), roll(v1, off)
            p0, p1, po = prev
            cols.append(jnp.where(lane8 < po, p0, jnp.where(lane8 < po + 32, p1, r0)))
            prev = (r0, r1, off)
            if off == 96:
                cols.append(jnp.where(lane8 < 96, r0, r1))
        for k in range(20):
            field_out[m, :, 128 * k:128 * (k + 1)] = cols[k].astype(BF16)

    for step in range(STEPS):
        by_side(lambda d: message(step, d).wait_send())


def per_device(field_state, reservoir_state, coupling_blocks, coupling_index, input_blocks, input_index, readout, region_band):
    smem = pl.BlockSpec(memory_space=pltpu.SMEM)
    hbm = pl.BlockSpec(memory_space=pl.ANY)
    vmem = pl.BlockSpec(memory_space=pltpu.VMEM)
    return pl.pallas_call(
        kernel,
        out_shape=(
            jax.ShapeDtypeStruct(field_state.shape, BF16),
            jax.ShapeDtypeStruct(reservoir_state.shape, BF16),
        ),
        in_specs=[smem] * 3 + [hbm] * 5,
        out_specs=(vmem, vmem),
        scratch_shapes=[
            pltpu.VMEM(field_state.shape, BF16),
            pltpu.VMEM(reservoir_state.shape, BF16),
            pltpu.VMEM(coupling_blocks.shape, BF16),
            pltpu.VMEM(input_blocks.shape, BF16),
            pltpu.VMEM(readout.shape, BF16),
            pltpu.VMEM((8, 128, 128), BF16),
            pltpu.VMEM((2, 8, 64, 128), F32),
            pltpu.VMEM((30, 64, 128), BF16),
            pltpu.VMEM((STEPS, 4, 3, 64, 128), BF16),
            pltpu.VMEM((STEPS, 2, 3, 64, 128), BF16),
            pltpu.VMEM((STEPS, 2, 3, 16, 128), BF16),
            pltpu.VMEM((STEPS, 8, 3, 16, 128), BF16),
            pltpu.VMEM((512, 128), F32),
            pltpu.VMEM((512, 128), F32),
            pltpu.SemaphoreType.DMA((5,)),
            pltpu.SemaphoreType.DMA((STEPS, 8)),
            pltpu.SemaphoreType.DMA((STEPS, 8)),
        ],
        compiler_params=pltpu.CompilerParams(
            collective_id=0, has_side_effects=True, vmem_limit_bytes=60 * 1024 * 1024
        ),
        name="forecast",
    )(
        jnp.swapaxes(coupling_index, 1, 2), input_index, region_band,
        field_state, reservoir_state, coupling_blocks, input_blocks, readout,
    )


def solution(mesh):
    return jax.shard_map(
        per_device,
        mesh=mesh,
        in_specs=(
            P(None, "lat", "lon"),
            P("lat", "lon", None, None),
            P("lat", None, None),
            P("lat", None, None),
            P("lat", None, None),
            P("lat", None),
            P("lat", None, None),
            P("lat"),
        ),
        out_specs=(P(None, "lat", "lon"), P("lat", "lon", None, None)),
        check_vma=False,
    )
```

time: 148 us -> 37.4 us (0.25)
  the two profiles are of different devices: /device:TPU:6 before, /device:TPU:8 now
where the time goes in v1:
time: 37.4 us; the launch traced here: 36.9 us
  Pallas kernels  32.9 us (88%)
  local copies, waits for them, and re-layouts  3.34 us (9%)
  between operations  0.64 us (2%)
    pallas_call x1, Pallas kernels, per_device(): pl.pallas_call(kernel, out_shape=(jax.ShapeDtypeStruct(field_state.shape,...  32.9 us
    unnamed x2, local copies, waits for them, and re-layouts  3.34 us

profile of v1, /device:TPU:8, one launch (start us, length us, event | category | flops | bytes accessed | tf_op | source)
XLA Modules:
  0.0 36.9 jit_solution(18240800282416863017)
XLA Ops:
  0.6 32.9 %forecast.1 = (bf16[4,8,2560]{2,1,0:T(8,128)(2,1)}, bf16[2,16,4,1024]{3,2,1,0:T(4,128)(2,1)}) custom-call(s32[2,2,8]{2,1,0:T(2,128)} %bitcast.1, s32[2,8]{1,0:T(2,128)} %qidx.1, s32[2]{0:T(128)} %rband.1, bf16[4,8,2560]{2,1,0:T(8,128)(2,1)} %field_hbm.1, bf16[2,16,4,1024]{3,2,1,0:T(4,128)(2,1)} %state_hbm.1, bf16[2,2048,128]{2,1,0:T(8,128)(2,1)} %coup_hbm.1, ...), custom_call_target="tpu_custom_call" | custom-call | tf_op jit(solution)/shard_map/forecast/pallas_call | solution.py:304
  33.6 1.6 %copy.12 = bf16[4,8,2560]{2,1,0:T(8,128)(2,1)} copy(bf16[4,8,2560]{2,1,0:T(8,128)(2,1)} %get-tuple-element.4) | data formatting | bytes 327680
  35.1 1.7 %copy.13 = bf16[2,16,4,1024]{3,2,1,0:T(4,128)(2,1)} copy(bf16[2,16,4,1024]{3,2,1,0:T(4,128)(2,1)} %get-tuple-element.5) | data formatting | bytes 524288

commit v2 on v1

--- a/solution.py
+++ b/solution.py
@@ -61,9 +61,10 @@
 
 
 def kernel(
-    cidx, qidx, rband,
+    cidx_hbm, qidx_hbm, rband_hbm,
     field_hbm, state_hbm, coup_hbm, drive_hbm, read_hbm,
     field_out, state_out,
+    cidx, qidx, rband,
     field_in, state_in, coup, drive, read,
     states, pre, win, raw, halo, edge, edge_in, ta, tb,
     local_sem, send_sem, recv_sem,
@@ -92,7 +93,8 @@
     loads = [
         pltpu.make_async_copy(src, dst, local_sem.at[n])
         for n, (src, dst) in enumerate(
-            ((field_hbm, field_in), (state_hbm, state_in), (coup_hbm, coup), (drive_hbm, drive), (read_hbm, read))
+            ((field_hbm, field_in), (state_hbm, state_in), (coup_hbm, coup), (drive_hbm, drive), (read_hbm, read),
+             (cidx_hbm, cidx), (qidx_hbm, qidx), (rband_hbm, rband))
         )
     ]
     for load in loads:
@@ -185,6 +187,8 @@
     loads[2].wait()
     loads[3].wait()
 
+    for load in loads[5:]:
+        load.wait()
     bands = [rband[i] for i in range(2)]
 
     for step in range(STEPS):
@@ -297,19 +301,32 @@
         by_side(lambda d: message(step, d).wait_send())
 
 
+def deliver(field_ref, state_ref, field_out, state_out, sems):
+    copies = [
+        pltpu.make_async_copy(field_ref, field_out, sems.at[0]),
+        pltpu.make_async_copy(state_ref, state_out, sems.at[1]),
+    ]
+    for copy in copies:
+        copy.start()
+    for copy in copies:
+        copy.wait()
+
+
 def per_device(field_state, reservoir_state, coupling_blocks, coupling_index, input_blocks, input_index, readout, region_band):
-    smem = pl.BlockSpec(memory_space=pltpu.SMEM)
-    hbm = pl.BlockSpec(memory_space=pl.ANY)
+    hbm = pl.BlockSpec(memory_space=pltpu.HBM)
     vmem = pl.BlockSpec(memory_space=pltpu.VMEM)
-    return pl.pallas_call(
+    field, state = pl.pallas_call(
         kernel,
         out_shape=(
-            jax.ShapeDtypeStruct(field_state.shape, BF16),
-            jax.ShapeDtypeStruct(reservoir_state.shape, BF16),
+            pltpu.VMEM(field_state.shape, BF16),
+            pltpu.VMEM(reservoir_state.shape, BF16),
         ),
-        in_specs=[smem] * 3 + [hbm] * 5,
+        in_specs=[hbm] * 8,
         out_specs=(vmem, vmem),
         scratch_shapes=[
+            pltpu.SMEM((2, 2, 8), jnp.int32),
+            pltpu.SMEM((2, 8), jnp.int32),
+            pltpu.SMEM((2,), jnp.int32),
             pltpu.VMEM(field_state.shape, BF16),
             pltpu.VMEM(reservoir_state.shape, BF16),
             pltpu.VMEM(coupling_blocks.shape, BF16),
@@ -324,18 +341,35 @@
             pltpu.VMEM((STEPS, 8, 3, 16, 128), BF16),
             pltpu.VMEM((512, 128), F32),
             pltpu.VMEM((512, 128), F32),
-            pltpu.SemaphoreType.DMA((5,)),
+            pltpu.SemaphoreType.DMA((8,)),
             pltpu.SemaphoreType.DMA((STEPS, 8)),
             pltpu.SemaphoreType.DMA((STEPS, 8)),
         ],
         compiler_params=pltpu.CompilerParams(
-            collective_id=0, has_side_effects=True, vmem_limit_bytes=60 * 1024 * 1024
+            collective_id=0, has_side_effects=True, vmem_limit_bytes=32 * 1024 * 1024
         ),
         name="forecast",
     )(
-        jnp.swapaxes(coupling_index, 1, 2), input_index, region_band,
-        field_state, reservoir_state, coupling_blocks, input_blocks, readout,
+        *(
+            pltpu.with_memory_space_constraint(x, pltpu.HBM)
+            for x in (
+                jnp.swapaxes(coupling_index, 1, 2), input_index, region_band,
+                field_state, reservoir_state, coupling_blocks, input_blocks, readout,
+            )
+        )
     )
+    return pl.pallas_call(
+        deliver,
+        out_shape=(
+            jax.ShapeDtypeStruct(field_state.shape, BF16),
+            jax.ShapeDtypeStruct(reservoir_state.shape, BF16),
+        ),
+        in_specs=[vmem] * 2,
+        out_specs=(hbm, hbm),
+        scratch_shapes=[pltpu.SemaphoreType.DMA((2,))],
+        compiler_params=pltpu.CompilerParams(vmem_limit_bytes=32 * 1024 * 1024),
+        name="deliver",
+    )(*(pltpu.with_memory_space_constraint(x, pltpu.VMEM) for x in (field, state)))
 
 
 def solution(mesh):

time: 37.4 us -> 33.3 us (0.89)
  local copies, waits for them, and re-layouts: 3.34 us -> 0 us
  Pallas kernels: 32.9 us -> 32.3 us
    unnamed x2 -> x0, local copies, waits for them, and re-layouts: 3.34 us -> none
    pallas_call x1 -> x2, Pallas kernels: 32.9 us -> 32.3 us  [the longest x1 31.5 us: per_device(): pl.pallas_call(kernel, out_shape=(pltpu.VMEM(field_state.shape, BF16), pl...]
where the time goes in v2:
time: 33.3 us; the launch traced here: 32.9 us
  Pallas kernels  32.3 us (97%)
  between operations  0.64 us (2%)
    pallas_call x1, Pallas kernels, per_device(): pl.pallas_call(kernel, out_shape=(pltpu.VMEM(field_state.shape, BF16), pl...  31.5 us
    pallas_call x1, Pallas kernels, per_device(): pl.pallas_call(deliver, out_shape=(jax.ShapeDtypeStruct(field_state.shape...  0.78 us

profile of v2, /device:TPU:8, one launch (start us, length us, event | category | flops | bytes accessed | tf_op | source)
XLA Modules:
  0.0 32.9 jit_solution(10792533761557631140)
XLA Ops:
  0.6 31.5 %forecast.1 = (bf16[4,8,2560]{2,1,0:T(8,128)(2,1)S(1)}, bf16[2,16,4,1024]{3,2,1,0:T(4,128)(2,1)S(1)}) custom-call(s32[2,2,8]{2,1,0:T(2,128)} %bitcast.1, s32[2,8]{1,0:T(2,128)} %qidx_hbm.1, s32[2]{0:T(128)} %rband_hbm.1, bf16[4,8,2560]{2,1,0:T(8,128)(2,1)} %field_hbm.1, bf16[2,16,4,1024]{3,2,1,0:T(4,128)(2,1)} %state_hbm.1, bf16[2,2048,128]{2,1,0:T(8,128)(2,1)} %coup_hbm.1, ...), custom_call_target="tpu_custom_call" | custom-call | tf_op jit(solution)/shard_map/forecast/pallas_call | solution.py:318
  32.1 0.8 %deliver.1 = (bf16[4,8,2560]{2,1,0:T(8,128)(2,1)}, bf16[2,16,4,1024]{3,2,1,0:T(4,128)(2,1)}) custom-call(bf16[4,8,2560]{2,1,0:T(8,128)(2,1)S(1)} %get-tuple-element.4.field_ref, bf16[2,16,4,1024]{3,2,1,0:T(4,128)(2,1)S(1)} %get-tuple-element.5.state_ref), custom_call_target="tpu_custom_call" | custom-call | tf_op jit(solution)/shard_map/deliver/pallas_call | solution.py:361

commit v3 on v2

v3 whole, which is shorter than its diff:
```python
import functools

import jax
import jax.numpy as jnp
from jax import lax
from jax.experimental import pallas as pl
from jax.experimental.pallas import tpu as pltpu
from jax.sharding import PartitionSpec as P

MESH = pl.DeviceIdType.MESH
STEPS = 3
F32 = jnp.float32
BF16 = jnp.bfloat16
TILES = 10
ROWS = 8 * TILES

DIRS = ((-1, 0), (1, 0), (0, -1), (0, 1), (-1, -1), (-1, 1), (1, -1), (1, 1))


def dot_nt(x, w):
    return lax.dot_general(x, w, (((1,), (1,)), ((), ())), preferred_element_type=F32)


def row_of(column, member):
    at = column + 2
    return at % TILES * 8 + at // TILES * 4 + member


def lanes(rows):
    return lax.broadcasted_iota(jnp.int32, (rows, 128), 1)


def roll(x, by):
    return pltpu.roll(x, by, 1)


def minus_parts(r0, r1, r2):
    lane = lanes(r0.shape[0])
    b0 = jnp.where(lane < 48, roll(r0, 48), roll(r1, 48))
    r2r = roll(r2, 80)
    b2 = jnp.where(lane < 80, roll(r1, 80), r2r)
    return b0, b2, r2r


def plus_parts(r0, r1):
    r0r = roll(r0, 112)
    return r0r, r0r, roll(r1, 16)


def windows(r0, r1, r2, n):
    rows = 8 * n
    lane = lanes(rows)
    m = slice(0, rows)
    c = slice(8, rows + 8)
    p = slice(16, rows + 16)
    m0, m2, m3 = minus_parts(r0[m], r1[m], r2[m])
    p1, p2, p4 = plus_parts(r0[p], r1[p])
    c0 = roll(r0[c], 80)
    c1 = roll(r1[c], 80)
    d1 = roll(r1[c], 112)
    d2 = roll(r2[c], 112)
    b0 = jnp.where(lane < 80, m0, c0)
    b1 = jnp.where(lane < 80, c0, jnp.where(lane < 112, c1, p1))
    b2 = jnp.where(lane < 64, p2, m2)
    b3 = jnp.where(lane < 16, m3, jnp.where(lane < 112, d1, d2))
    b4 = jnp.where(lane < 48, d2, p4)
    return b0, b1, b2, b3, b4


def kernel(
    cidx_hbm, qidx_hbm, rband_hbm,
    field_hbm, state_hbm, coup_hbm, drive_hbm, read_hbm,
    field_out, state_out,
    cidx, qidx, rband,
    field_in, state_in, coup, drive, read,
    states, pre, win, raw, halo, edge, edge_in, state_edge, ta, tb,
    local_sem, send_sem, recv_sem,
):
    lat, lon = lax.axis_index("lat"), lax.axis_index("lon")
    nlat, nlon = lax.axis_size("lat"), lax.axis_size("lon")
    west, east = lax.rem(lon + nlon - 1, nlon), lax.rem(lon + 1, nlon)
    has_south = lat > 0
    has_north = lat < nlat - 1

    def target(d):
        dl, do = DIRS[d]
        return (lat + dl, west if do < 0 else (east if do > 0 else lon))

    def by_side(fn, dirs=range(8)):
        for d in dirs:
            dl = DIRS[d][0]
            if dl == 0:
                fn(d)
            else:
                pl.when(has_south if dl < 0 else has_north)(functools.partial(fn, d))

    barrier = pltpu.get_barrier_semaphore()
    by_side(
        lambda d: pl.semaphore_signal(barrier, inc=1, device_id=target(d), device_id_type=MESH),
        (4, 5, 6, 7, 2, 3, 0, 1),
    )

    loads = [
        pltpu.make_async_copy(src, dst, local_sem.at[n])
        for n, (src, dst) in enumerate(
            ((field_hbm, field_in), (state_hbm, state_in), (coup_hbm, coup), (drive_hbm, drive), (read_hbm, read),
             (cidx_hbm, cidx), (qidx_hbm, qidx), (rband_hbm, rband))
        )
    ]
    for load in loads:
        load.start()

    @pl.when(lat == 0)
    def _():
        halo[:, 0] = jnp.zeros(halo.shape[:1] + halo.shape[2:], BF16)
        edge_in[2:4, 3] = jnp.zeros((2,) + edge_in.shape[2:], BF16)

    @pl.when(lat == nlat - 1)
    def _():
        halo[:, 1] = jnp.zeros(halo.shape[:1] + halo.shape[2:], BF16)
        edge_in[2:4, 0] = jnp.zeros((2,) + edge_in.shape[2:], BF16)

    def remote(src, dst, step, n, d):
        return pltpu.make_async_remote_copy(
            src_ref=src, dst_ref=dst, send_sem=send_sem.at[step, n], recv_sem=recv_sem.at[step, n],
            device_id=target(d), device_id_type=MESH,
        )

    def message(step, d):
        if d == 0:
            return remote(raw.at[step, 0], halo.at[step, 1], step, d, d)
        if d == 1:
            return remote(raw.at[step, 3], halo.at[step, 0], step, d, d)
        dl, do = DIRS[d]
        side, into = (0, 1) if do < 0 else (1, 0)
        if dl == 0:
            return remote(edge.at[side], edge_in.at[into], step, d, d)
        pair = 0 if dl < 0 else 3
        return remote(edge.at[side, pair], edge_in.at[2 + into, pair], step, d, d)

    def state_message(d):
        side, into = (0, 1) if DIRS[d][1] < 0 else (1, 0)
        return remote(state_hbm.at[:, pl.ds(14 * side, 2)], state_edge.at[into], 0, 6 + d, d)

    def wait_recv(step, dirs):
        for d in dirs:
            dl = DIRS[d][0]
            if dl == 0:
                message(step, d).wait_recv()
            else:
                pl.when(has_north if dl < 0 else has_south)(message(step, d).wait_recv)

    def put_raw(step, pair, r):
        for k in range(3):
            raw[step, pair, k] = r[k].astype(BF16)

    loads[0].wait()
    lane8 = lanes(8)
    for m in range(4):
        f = [field_in[m, :, 128 * k:128 * (k + 1)].astype(F32) for k in range(20)]
        for j in range(16):
            q, off = (160 * j) // 128, (160 * j) % 128
            if off == 0:
                w0, w1 = f[q], f[q + 1]
            else:
                w1 = roll(f[q + 1], 128 - off)
                w0 = jnp.where(lane8 < 128 - off, roll(f[q], 128 - off), w1)
            ta[pl.ds(row_of(j, m), 8, stride=ROWS), :] = w0
            tb[pl.ds(row_of(j, m), 8, stride=ROWS), :] = w1
    lane_all = lanes(ROWS)
    for p in range(4):
        lo, mid, hi = 2 * p * ROWS, (2 * p + 1) * ROWS, (2 * p + 2) * ROWS
        a0, a1 = ta[lo:mid], tb[lo:mid]
        b0, b1 = roll(ta[mid:hi], 32), roll(tb[mid:hi], 32)
        r = (a0, jnp.where(lane_all < 32, a1, b0), jnp.where(lane_all < 32, b0, b1))
        put_raw(0, p, r)
        for k in range(3):
            for side, cols in enumerate(((0, 1, 2), (13, 14, 15))):
                at = [row_of(j, 0) for j in cols]
                at.append(at[0])
                rows = jnp.concatenate([r[k][x:x + 4] for x in at], axis=0)
                edge[side, p, k] = rows.astype(BF16)

    pl.semaphore_wait(
        barrier, 2 + 3 * has_south.astype(jnp.int32) + 3 * has_north.astype(jnp.int32)
    )
    by_side(lambda d: message(0, d).start(), (4, 5, 6, 7, 2, 3))
    for d in (2, 3):
        state_message(d).start()
    by_side(lambda d: message(0, d).start(), (0, 1))

    def put_state(i, t):
        tiles = []
        for s in (t, t + 1):
            tiles.append(state_in[i, s - 2] if s >= 2 else state_edge[0, i, s])
            tiles.append(state_in[i, s + 8] if s < 8 else state_edge[1, i, s - 8])
        rows = jnp.concatenate([x.astype(F32) for x in tiles], axis=0).astype(BF16)
        for c in range(8):
            states[c, ROWS * i + 8 * t:ROWS * i + 8 * t + 16] = rows[:, 128 * c:128 * (c + 1)]

    loads[1].wait()
    for i in range(2):
        for t in (2, 4, 6):
            put_state(i, t)
    for load in loads[2:4] + loads[5:]:
        load.wait()
    bands = [rband[i] for i in range(2)]

    def put_windows(at, ext):
        for k, block in enumerate(windows(*ext, TILES)):
            win[at + k] = block.astype(BF16)

    def with_edges(r, w, x):
        return jnp.concatenate(
            [
                w[0:4], r[72:76], w[4:8], r[4:8], w[8:12], r[12:16],
                r[16:64],
                r[64:68], x[0:4], r[72:76], x[4:8], r[4:8], x[8:12],
            ],
            axis=0,
        )

    def without_edges(r):
        return jnp.concatenate([r[72:76], r[72:76], r, r[4:8], r[4:8]], axis=0)

    for step in range(STEPS):
        if step == 0:
            for d in (2, 3):
                state_message(d).wait_recv()
            for i in range(2):
                for t in (0, 8):
                    put_state(i, t)
        for i in range(2):
            for b in range(8):
                x = jnp.concatenate(
                    [states[cidx[bands[i], k, b], ROWS * i:ROWS * (i + 1)] for k in range(2)], axis=1
                )
                w = jnp.concatenate(
                    [coup[bands[i], (2 * b + k) * 128:(2 * b + k + 1) * 128] for k in range(2)], axis=1
                )
                pre[i, b] = dot_nt(x, w)
        if step == 0:
            wait_recv(step, (2, 3))
        for p in range(4):
            ext = []
            for k in range(3):
                r = raw[step, p, k].astype(F32)
                if step == 0:
                    w, x = (edge_in[side, p, k].astype(F32) for side in range(2))
                    ext.append(with_edges(r, w, x))
                else:
                    ext.append(without_edges(r))
            put_windows(5 + 5 * p, ext)

        wait_recv(step, (0, 1) + ((4, 5, 6, 7) if step == 0 else ()))
        for side, p in enumerate((3, 0)):
            ext = []
            for k in range(3):
                r = halo[step, side, k].astype(F32)
                if step == 0:
                    w, x = (edge_in[2 + s, p, k].astype(F32) for s in range(2))
                    ext.append(with_edges(r, w, x))
                else:
                    ext.append(without_edges(r))
            put_windows(25 * side, ext)

        for i in range(2):
            for b in range(8):
                x = win[10 * i + qidx[bands[i], b]]
                w = drive[bands[i], 128 * b:128 * (b + 1)]
                new = jnp.tanh(pre[i, b] + dot_nt(x, w))
                states[b, ROWS * i:ROWS * (i + 1)] = new.astype(BF16)
                if step == STEPS - 1:
                    for j in range(16):
                        at = row_of(j, 0)
                        state_out[i, j, :, 128 * b:128 * (b + 1)] = new[at:at + 4].astype(BF16)
        if step == 0:
            loads[4].wait()
        x = jnp.concatenate([states[c] for c in range(8)], axis=1)
        if step < STEPS - 1:
            for h in range(2):
                y = dot_nt(x, read[0, 320 * h:320 * h + 320])
                y = jnp.concatenate([y, jnp.zeros((2 * ROWS, 64), F32)], axis=1)
                for i in range(2):
                    put_raw(
                        step + 1, 2 * i + h,
                        tuple(y[ROWS * i:ROWS * (i + 1), 128 * k:128 * (k + 1)] for k in range(3)),
                    )
                by_side(lambda d: message(step + 1, d).start(), (h,))
        else:
            for dy in range(4):
                y = dot_nt(x, read[0, 160 * dy:160 * dy + 160])
                for i in range(2):
                    at = ROWS * (4 * i + dy)
                    ta[at:at + ROWS] = y[ROWS * i:ROWS * (i + 1), 0:128]
                    tb[at:at + ROWS, 0:32] = y[ROWS * i:ROWS * (i + 1), 128:160]

    for m in range(4):
        cols = []
        prev = None
        for j in range(16):
            off = (160 * j) % 128
            v0 = ta[pl.ds(row_of(j, m), 8, stride=ROWS), :]
            v1 = tb[pl.ds(row_of(j, m), 8, stride=ROWS), :]
            if off == 0:
                cols.append(v0)
                prev = (v0, v1, 0)
                continue
            r0, r1 = roll(v0, off), roll(v1, off)
            p0, p1, po = prev
            cols.append(jnp.where(lane8 < po, p0, jnp.where(lane8 < po + 32, p1, r0)))
            prev = (r0, r1, off)
            if off == 96:
                cols.append(jnp.where(lane8 < 96, r0, r1))
        for k in range(20):
            field_out[m, :, 128 * k:128 * (k + 1)] = cols[k].astype(BF16)

    by_side(lambda d: message(0, d).wait_send())
    for d in (2, 3):
        state_message(d).wait_send()
    for step in range(1, STEPS):
        by_side(lambda d: message(step, d).wait_send(), (0, 1))


def deliver(field_ref, state_ref, field_out, state_out, sems):
    copies = [
        pltpu.make_async_copy(field_ref, field_out, sems.at[0]),
        pltpu.make_async_copy(state_ref, state_out, sems.at[1]),
    ]
    for copy in copies:
        copy.start()
    for copy in copies:
        copy.wait()


def per_device(field_state, reservoir_state, coupling_blocks, coupling_index, input_blocks, input_index, readout, region_band):
    hbm = pl.BlockSpec(memory_space=pltpu.HBM)
    vmem = pl.BlockSpec(memory_space=pltpu.VMEM)
    field, state = pl.pallas_call(
        kernel,
        out_shape=(
            pltpu.VMEM(field_state.shape, BF16),
            pltpu.VMEM(reservoir_state.shape, BF16),
        ),
        in_specs=[hbm] * 8,
        out_specs=(vmem, vmem),
        scratch_shapes=[
            pltpu.SMEM((2, 2, 8), jnp.int32),
            pltpu.SMEM((2, 8), jnp.int32),
            pltpu.SMEM((2,), jnp.int32),
            pltpu.VMEM(field_state.shape, BF16),
            pltpu.VMEM(reservoir_state.shape, BF16),
            pltpu.VMEM(coupling_blocks.shape, BF16),
            pltpu.VMEM(input_blocks.shape, BF16),
            pltpu.VMEM(readout.shape, BF16),
            pltpu.VMEM((8, 2 * ROWS, 128), BF16),
            pltpu.VMEM((2, 8, ROWS, 128), F32),
            pltpu.VMEM((30, ROWS, 128), BF16),
            pltpu.VMEM((STEPS, 4, 3, ROWS, 128), BF16),
            pltpu.VMEM((STEPS, 2, 3, ROWS, 128), BF16),
            pltpu.VMEM((2, 4, 3, 16, 128), BF16),
            pltpu.VMEM((4, 4, 3, 16, 128), BF16),
            pltpu.VMEM((2, 2, 2, 4, 1024), BF16),
            pltpu.VMEM((8 * ROWS, 128), F32),
            pltpu.VMEM((8 * ROWS, 128), F32),
            pltpu.SemaphoreType.DMA((8,)),
            pltpu.SemaphoreType.DMA((STEPS, 10)),
            pltpu.SemaphoreType.DMA((STEPS, 10)),
        ],
        compiler_params=pltpu.CompilerParams(
            collective_id=0, has_side_effects=True, vmem_limit_bytes=32 * 1024 * 1024
        ),
        name="forecast",
    )(
        *(
            pltpu.with_memory_space_constraint(x, pltpu.HBM)
            for x in (
                jnp.swapaxes(coupling_index, 1, 2), input_index, region_band,
                field_state, reservoir_state, coupling_blocks, input_blocks, readout,
            )
        )
    )
    return pl.pallas_call(
        deliver,
        out_shape=(
            jax.ShapeDtypeStruct(field_state.shape, BF16),
            jax.ShapeDtypeStruct(reservoir_state.shape, BF16),
        ),
        in_specs=[vmem] * 2,
        out_specs=(hbm, hbm),
        scratch_shapes=[pltpu.SemaphoreType.DMA((2,))],
        compiler_params=pltpu.CompilerParams(vmem_limit_bytes=32 * 1024 * 1024),
        name="deliver",
    )(*(pltpu.with_memory_space_constraint(x, pltpu.VMEM) for x in (field, state)))


def solution(mesh):
    return jax.shard_map(
        per_device,
        mesh=mesh,
        in_specs=(
            P(None, "lat", "lon"),
            P("lat", "lon", None, None),
            P("lat", None, None),
            P("lat", None, None),
            P("lat", None, None),
            P("lat", None),
            P("lat", None, None),
            P("lat"),
        ),
        out_specs=(P(None, "lat", "lon"), P("lat", "lon", None, None)),
        check_vma=False,
    )
```

time: 33.3 us -> 32 us (0.961)
  Pallas kernels: 32.3 us -> 31.2 us
    pallas_call x1, Pallas kernels: 31.5 us -> 30.5 us  [per_device(): pl.pallas_call(kernel, out_shape=(pltpu.VMEM(field_state.shape, BF16), pl...]
where the time goes in v3:
time: 32 us; the launch traced here: 31.9 us
  Pallas kernels  31.2 us (98%)
  between operations  0.64 us (2%)
    pallas_call x1, Pallas kernels, per_device(): pl.pallas_call(kernel, out_shape=(pltpu.VMEM(field_state.shape, BF16), pl...  30.5 us
    pallas_call x1, Pallas kernels, per_device(): pl.pallas_call(deliver, out_shape=(jax.ShapeDtypeStruct(field_state.shape...  0.78 us

profile of v3, /device:TPU:8, one launch (start us, length us, event | category | flops | bytes accessed | tf_op | source)
XLA Modules:
  0.0 31.9 jit_solution(16354923006500709371)
XLA Ops:
  0.6 30.5 %forecast.1 = (bf16[4,8,2560]{2,1,0:T(8,128)(2,1)S(1)}, bf16[2,16,4,1024]{3,2,1,0:T(4,128)(2,1)S(1)}) custom-call(s32[2,2,8]{2,1,0:T(2,128)} %bitcast.1, s32[2,8]{1,0:T(2,128)} %qidx_hbm.1, s32[2]{0:T(128)} %rband_hbm.1, bf16[4,8,2560]{2,1,0:T(8,128)(2,1)} %field_hbm.1, bf16[2,16,4,1024]{3,2,1,0:T(4,128)(2,1)} %state_hbm.1, bf16[2,2048,128]{2,1,0:T(8,128)(2,1)} %coup_hbm.1, ...), custom_call_target="tpu_custom_call" | custom-call | tf_op jit(solution)/shard_map/forecast/pallas_call | solution.py:339
  31.1 0.8 %deliver.1 = (bf16[4,8,2560]{2,1,0:T(8,128)(2,1)}, bf16[2,16,4,1024]{3,2,1,0:T(4,128)(2,1)}) custom-call(bf16[4,8,2560]{2,1,0:T(8,128)(2,1)S(1)} %get-tuple-element.4.field_ref, bf16[2,16,4,1024]{3,2,1,0:T(4,128)(2,1)S(1)} %get-tuple-element.5.state_ref), custom_call_target="tpu_custom_call" | custom-call | tf_op jit(solution)/shard_map/deliver/pallas_call | solution.py:383

commit v4 on v3

--- a/solution.py
+++ b/solution.py
@@ -74,7 +74,7 @@
     cidx, qidx, rband,
     field_in, state_in, coup, drive, read,
     states, pre, win, raw, halo, edge, edge_in, state_edge, ta, tb,
-    local_sem, send_sem, recv_sem,
+    local_sem, send_sem, recv_sem, ready,
 ):
     lat, lon = lax.axis_index("lat"), lax.axis_index("lon")
     nlat, nlon = lax.axis_size("lat"), lax.axis_size("lon")
@@ -94,11 +94,22 @@
             else:
                 pl.when(has_south if dl < 0 else has_north)(functools.partial(fn, d))
 
+    is_first = lon == 0
+    is_last = lon == nlon - 1
+    is_before_last = lon == nlon - 2
+    greeted = 1 + has_south.astype(jnp.int32) + has_north.astype(jnp.int32)
+
     barrier = pltpu.get_barrier_semaphore()
-    by_side(
-        lambda d: pl.semaphore_signal(barrier, inc=1, device_id=target(d), device_id_type=MESH),
-        (4, 5, 6, 7, 2, 3, 0, 1),
-    )
+
+    def greet(d):
+        pl.semaphore_signal(barrier, inc=1, device_id=target(d), device_id_type=MESH)
+
+    by_side(greet, (4, 6, 2))
+
+    @pl.when(jnp.logical_not(is_last))
+    def _():
+        by_side(greet, (0, 1))
+        pl.when(jnp.logical_not(is_before_last))(lambda: by_side(greet, (5, 7, 3)))
 
     loads = [
         pltpu.make_async_copy(src, dst, local_sem.at[n])
@@ -153,6 +164,11 @@
     def put_raw(step, pair, r):
         for k in range(3):
             raw[step, pair, k] = r[k].astype(BF16)
+
+    @pl.when(is_last)
+    def _():
+        pl.semaphore_wait(barrier, greeted)
+        state_message(3).start()
 
     loads[0].wait()
     lane8 = lanes(8)
@@ -181,13 +197,32 @@
                 rows = jnp.concatenate([r[k][x:x + 4] for x in at], axis=0)
                 edge[side, p, k] = rows.astype(BF16)
 
-    pl.semaphore_wait(
-        barrier, 2 + 3 * has_south.astype(jnp.int32) + 3 * has_north.astype(jnp.int32)
-    )
-    by_side(lambda d: message(0, d).start(), (4, 5, 6, 7, 2, 3))
-    for d in (2, 3):
-        state_message(d).start()
-    by_side(lambda d: message(0, d).start(), (0, 1))
+    def start(d):
+        message(0, d).start()
+
+    def send_west():
+        by_side(start, (4, 6, 2))
+        state_message(2).start()
+
+    @pl.when(is_last)
+    def _():
+        by_side(start, (5, 7, 3))
+        pl.semaphore_wait(ready, 1)
+        by_side(start, (0, 1))
+        send_west()
+
+    @pl.when(jnp.logical_not(is_last))
+    def _():
+        pl.semaphore_wait(barrier, 2 * greeted - 1 + jnp.where(is_first, 0, greeted))
+
+        @pl.when(is_before_last)
+        def _():
+            pl.semaphore_signal(ready, inc=1, device_id=(lat, east), device_id_type=MESH)
+
+        by_side(start, (5, 7, 3))
+        state_message(3).start()
+        by_side(start, (0, 1))
+        pl.when(jnp.logical_not(is_first))(send_west)
 
     def put_state(i, t):
         tiles = []
@@ -240,7 +275,9 @@
                 )
                 pre[i, b] = dot_nt(x, w)
         if step == 0:
-            wait_recv(step, (2, 3))
+            wait_recv(step, (3, 5, 7))
+            pl.when(is_first)(send_west)
+            wait_recv(step, (2,))
         for p in range(4):
             ext = []
             for k in range(3):
@@ -252,7 +289,7 @@
                     ext.append(without_edges(r))
             put_windows(5 + 5 * p, ext)
 
-        wait_recv(step, (0, 1) + ((4, 5, 6, 7) if step == 0 else ()))
+        wait_recv(step, (0, 1) + ((4, 6) if step == 0 else ()))
         for side, p in enumerate((3, 0)):
             ext = []
             for k in range(3):
@@ -366,6 +403,7 @@
             pltpu.SemaphoreType.DMA((8,)),
             pltpu.SemaphoreType.DMA((STEPS, 10)),
             pltpu.SemaphoreType.DMA((STEPS, 10)),
+            pltpu.SemaphoreType.REGULAR,
         ],
         compiler_params=pltpu.CompilerParams(
             collective_id=0, has_side_effects=True, vmem_limit_bytes=32 * 1024 * 1024

time: 32 us -> 30.4 us (0.950)
  Pallas kernels: 31.2 us -> 29.6 us
    pallas_call x1, Pallas kernels: 30.5 us -> 28.9 us  [per_device(): pl.pallas_call(kernel, out_shape=(pltpu.VMEM(field_state.shape, BF16), pl...]
where the time goes in v4:
time: 30.4 us; the launch traced here: 30.3 us
  Pallas kernels  29.6 us (97%)
  between operations  0.64 us (2%)
    pallas_call x1, Pallas kernels, per_device(): pl.pallas_call(kernel, out_shape=(pltpu.VMEM(field_state.shape, BF16), pl...  28.9 us
    pallas_call x1, Pallas kernels, per_device(): pl.pallas_call(deliver, out_shape=(jax.ShapeDtypeStruct(field_state.shape...  0.78 us

profile of v4, /device:TPU:8, one launch (start us, length us, event | category | flops | bytes accessed | tf_op | source)
XLA Modules:
  0.0 30.3 jit_solution(4691675033247406649)
XLA Ops:
  0.6 28.9 %forecast.1 = (bf16[4,8,2560]{2,1,0:T(8,128)(2,1)S(1)}, bf16[2,16,4,1024]{3,2,1,0:T(4,128)(2,1)S(1)}) custom-call(s32[2,2,8]{2,1,0:T(2,128)} %bitcast.1, s32[2,8]{1,0:T(2,128)} %qidx_hbm.1, s32[2]{0:T(128)} %rband_hbm.1, bf16[4,8,2560]{2,1,0:T(8,128)(2,1)} %field_hbm.1, bf16[2,16,4,1024]{3,2,1,0:T(4,128)(2,1)} %state_hbm.1, bf16[2,2048,128]{2,1,0:T(8,128)(2,1)} %coup_hbm.1, ...), custom_call_target="tpu_custom_call" | custom-call | tf_op jit(solution)/shard_map/forecast/pallas_call | solution.py:376
  29.5 0.8 %deliver.1 = (bf16[4,8,2560]{2,1,0:T(8,128)(2,1)}, bf16[2,16,4,1024]{3,2,1,0:T(4,128)(2,1)}) custom-call(bf16[4,8,2560]{2,1,0:T(8,128)(2,1)S(1)} %get-tuple-element.4.field_ref, bf16[2,16,4,1024]{3,2,1,0:T(4,128)(2,1)S(1)} %get-tuple-element.5.state_ref), custom_call_target="tpu_custom_call" | custom-call | tf_op jit(solution)/shard_map/deliver/pallas_call | solution.py:421

commit v5 on v4

--- a/solution.py
+++ b/solution.py
@@ -73,7 +73,7 @@
     field_out, state_out,
     cidx, qidx, rband,
     field_in, state_in, coup, drive, read,
-    states, pre, win, raw, halo, edge, edge_in, state_edge, ta, tb,
+    states, pre, win, raw, halo, edge, edge_in, state_edge, ta, tb, ea, eb,
     local_sem, send_sem, recv_sem, ready,
 ):
     lat, lon = lax.axis_index("lat"), lax.axis_index("lon")
@@ -114,22 +114,14 @@
     loads = [
         pltpu.make_async_copy(src, dst, local_sem.at[n])
         for n, (src, dst) in enumerate(
-            ((field_hbm, field_in), (state_hbm, state_in), (coup_hbm, coup), (drive_hbm, drive), (read_hbm, read),
+            ((field_hbm.at[:, :, 2048:2560], field_in.at[:, :, 2048:2560]),
+             (field_hbm.at[:, :, 0:2048], field_in.at[:, :, 0:2048]),
+             (state_hbm, state_in), (coup_hbm, coup), (drive_hbm, drive), (read_hbm, read),
              (cidx_hbm, cidx), (qidx_hbm, qidx), (rband_hbm, rband))
         )
     ]
     for load in loads:
         load.start()
-
-    @pl.when(lat == 0)
-    def _():
-        halo[:, 0] = jnp.zeros(halo.shape[:1] + halo.shape[2:], BF16)
-        edge_in[2:4, 3] = jnp.zeros((2,) + edge_in.shape[2:], BF16)
-
-    @pl.when(lat == nlat - 1)
-    def _():
-        halo[:, 1] = jnp.zeros(halo.shape[:1] + halo.shape[2:], BF16)
-        edge_in[2:4, 0] = jnp.zeros((2,) + edge_in.shape[2:], BF16)
 
     def remote(src, dst, step, n, d):
         return pltpu.make_async_remote_copy(
@@ -170,35 +162,58 @@
         pl.semaphore_wait(barrier, greeted)
         state_message(3).start()
 
-    loads[0].wait()
     lane8 = lanes(8)
-    for m in range(4):
-        f = [field_in[m, :, 128 * k:128 * (k + 1)].astype(F32) for k in range(20)]
-        for j in range(16):
-            q, off = (160 * j) // 128, (160 * j) % 128
-            if off == 0:
-                w0, w1 = f[q], f[q + 1]
-            else:
-                w1 = roll(f[q + 1], 128 - off)
-                w0 = jnp.where(lane8 < 128 - off, roll(f[q], 128 - off), w1)
-            ta[pl.ds(row_of(j, m), 8, stride=ROWS), :] = w0
-            tb[pl.ds(row_of(j, m), 8, stride=ROWS), :] = w1
-    lane_all = lanes(ROWS)
-    for p in range(4):
-        lo, mid, hi = 2 * p * ROWS, (2 * p + 1) * ROWS, (2 * p + 2) * ROWS
-        a0, a1 = ta[lo:mid], tb[lo:mid]
-        b0, b1 = roll(ta[mid:hi], 32), roll(tb[mid:hi], 32)
-        r = (a0, jnp.where(lane_all < 32, a1, b0), jnp.where(lane_all < 32, b0, b1))
-        put_raw(0, p, r)
-        for k in range(3):
-            for side, cols in enumerate(((0, 1, 2), (13, 14, 15))):
-                at = [row_of(j, 0) for j in cols]
-                at.append(at[0])
-                rows = jnp.concatenate([r[k][x:x + 4] for x in at], axis=0)
+
+    def to_regions(columns, row, stride, to_a, to_b):
+        for m in range(4):
+            f = {}
+            for j in columns:
+                q, off = (160 * j) // 128, (160 * j) % 128
+                for k in (q, q + 1):
+                    if k not in f:
+                        f[k] = field_in[m, :, 128 * k:128 * (k + 1)].astype(F32)
+                if off == 0:
+                    w0, w1 = f[q], f[q + 1]
+                else:
+                    w1 = roll(f[q + 1], 128 - off)
+                    w0 = jnp.where(lane8 < 128 - off, roll(f[q], 128 - off), w1)
+                to_a[pl.ds(row(j, m), 8, stride=stride), :] = w0
+                to_b[pl.ds(row(j, m), 8, stride=stride), :] = w1
+
+    def to_pair(p, rows, from_a, from_b):
+        lane = lanes(rows)
+        lo, mid, hi = 2 * p * rows, (2 * p + 1) * rows, (2 * p + 2) * rows
+        a0, a1 = from_a[lo:mid], from_b[lo:mid]
+        b0, b1 = roll(from_a[mid:hi], 32), roll(from_b[mid:hi], 32)
+        return a0, jnp.where(lane < 32, a1, b0), jnp.where(lane < 32, b0, b1)
+
+    def put_edge(side, first):
+        to_regions(range(first, first + 3), lambda j, m: 4 * (j - first) + m, 16, ea.at[side], eb.at[side])
+        for p in range(4):
+            for k, rows in enumerate(to_pair(p, 16, ea.at[side], eb.at[side])):
                 edge[side, p, k] = rows.astype(BF16)
 
     def start(d):
         message(0, d).start()
+
+    loads[0].wait()
+    put_edge(1, 13)
+    pl.when(is_last)(lambda: by_side(start, (5, 7, 3)))
+    loads[1].wait()
+    put_edge(0, 0)
+    to_regions(range(16), row_of, ROWS, ta, tb)
+    for p in range(4):
+        put_raw(0, p, to_pair(p, ROWS, ta, tb))
+
+    @pl.when(lat == 0)
+    def _():
+        halo[:, 0] = jnp.zeros(halo.shape[:1] + halo.shape[2:], BF16)
+        edge_in[2:4, 3] = jnp.zeros((2,) + edge_in.shape[2:], BF16)
+
+    @pl.when(lat == nlat - 1)
+    def _():
+        halo[:, 1] = jnp.zeros(halo.shape[:1] + halo.shape[2:], BF16)
+        edge_in[2:4, 0] = jnp.zeros((2,) + edge_in.shape[2:], BF16)
 
     def send_west():
         by_side(start, (4, 6, 2))
@@ -206,7 +221,6 @@
 
     @pl.when(is_last)
     def _():
-        by_side(start, (5, 7, 3))
         pl.semaphore_wait(ready, 1)
         by_side(start, (0, 1))
         send_west()
@@ -233,11 +247,11 @@
         for c in range(8):
             states[c, ROWS * i + 8 * t:ROWS * i + 8 * t + 16] = rows[:, 128 * c:128 * (c + 1)]
 
-    loads[1].wait()
+    loads[2].wait()
     for i in range(2):
         for t in (2, 4, 6):
             put_state(i, t)
-    for load in loads[2:4] + loads[5:]:
+    for load in loads[3:5] + loads[6:]:
         load.wait()
     bands = [rband[i] for i in range(2)]
 
@@ -312,18 +326,21 @@
                         at = row_of(j, 0)
                         state_out[i, j, :, 128 * b:128 * (b + 1)] = new[at:at + 4].astype(BF16)
         if step == 0:
-            loads[4].wait()
+            loads[5].wait()
         x = jnp.concatenate([states[c] for c in range(8)], axis=1)
         if step < STEPS - 1:
-            for h in range(2):
-                y = dot_nt(x, read[0, 320 * h:320 * h + 320])
+            first = jnp.where(lat < nlat // 2, 1, 0)
+            for n in range(2):
+                h = first if n == 0 else 1 - first
+                y = dot_nt(x, read[0, pl.ds(pl.multiple_of(320 * h, 320), 320)])
                 y = jnp.concatenate([y, jnp.zeros((2 * ROWS, 64), F32)], axis=1)
                 for i in range(2):
                     put_raw(
                         step + 1, 2 * i + h,
                         tuple(y[ROWS * i:ROWS * (i + 1), 128 * k:128 * (k + 1)] for k in range(3)),
                     )
-                by_side(lambda d: message(step + 1, d).start(), (h,))
+                pl.when((h == 0) & has_south)(message(step + 1, 0).start)
+                pl.when((h == 1) & has_north)(message(step + 1, 1).start)
         else:
             for dy in range(4):
                 y = dot_nt(x, read[0, 160 * dy:160 * dy + 160])
@@ -400,7 +417,9 @@
             pltpu.VMEM((2, 2, 2, 4, 1024), BF16),
             pltpu.VMEM((8 * ROWS, 128), F32),
             pltpu.VMEM((8 * ROWS, 128), F32),
-            pltpu.SemaphoreType.DMA((8,)),
+            pltpu.VMEM((2, 128, 128), F32),
+            pltpu.VMEM((2, 128, 128), F32),
+            pltpu.SemaphoreType.DMA((9,)),
             pltpu.SemaphoreType.DMA((STEPS, 10)),
             pltpu.SemaphoreType.DMA((STEPS, 10)),
             pltpu.SemaphoreType.REGULAR,

time: 30.4 us -> 29.6 us (0.974)
  Pallas kernels: 29.6 us -> 28.8 us
    pallas_call x1, Pallas kernels: 28.9 us -> 28.1 us  [per_device(): pl.pallas_call(kernel, out_shape=(pltpu.VMEM(field_state.shape, BF16), pl...]
where the time goes in v5:
time: 29.6 us; the launch traced here: 29.5 us
  Pallas kernels  28.8 us (97%)
  between operations  0.64 us (2%)
    pallas_call x1, Pallas kernels, per_device(): pl.pallas_call(kernel, out_shape=(pltpu.VMEM(field_state.shape, BF16), pl...  28.1 us
    pallas_call x1, Pallas kernels, per_device(): pl.pallas_call(deliver, out_shape=(jax.ShapeDtypeStruct(field_state.shape...  0.78 us

profile of v5, /device:TPU:8, one launch (start us, length us, event | category | flops | bytes accessed | tf_op | source)
XLA Modules:
  0.0 29.5 jit_solution(9176594828166266600)
XLA Ops:
  0.6 28.1 %forecast.1 = (bf16[4,8,2560]{2,1,0:T(8,128)(2,1)S(1)}, bf16[2,16,4,1024]{3,2,1,0:T(4,128)(2,1)S(1)}) custom-call(s32[2,2,8]{2,1,0:T(2,128)} %bitcast.1, s32[2,8]{1,0:T(2,128)} %qidx_hbm.1, s32[2]{0:T(128)} %rband_hbm.1, bf16[4,8,2560]{2,1,0:T(8,128)(2,1)} %field_hbm.1, bf16[2,16,4,1024]{3,2,1,0:T(4,128)(2,1)} %state_hbm.1, bf16[2,2048,128]{2,1,0:T(8,128)(2,1)} %coup_hbm.1, ...), custom_call_target="tpu_custom_call" | custom-call | tf_op jit(solution)/shard_map/forecast/pallas_call | solution.py:393
  28.7 0.8 %deliver.1 = (bf16[4,8,2560]{2,1,0:T(8,128)(2,1)}, bf16[2,16,4,1024]{3,2,1,0:T(4,128)(2,1)}) custom-call(bf16[4,8,2560]{2,1,0:T(8,128)(2,1)S(1)} %get-tuple-element.4.field_ref, bf16[2,16,4,1024]{3,2,1,0:T(4,128)(2,1)S(1)} %get-tuple-element.5.state_ref), custom_call_target="tpu_custom_call" | custom-call | tf_op jit(solution)/shard_map/deliver/pallas_call | solution.py:440

commit v6 on v5

--- a/solution.py
+++ b/solution.py
@@ -94,23 +94,6 @@
             else:
                 pl.when(has_south if dl < 0 else has_north)(functools.partial(fn, d))
 
-    is_first = lon == 0
-    is_last = lon == nlon - 1
-    is_before_last = lon == nlon - 2
-    greeted = 1 + has_south.astype(jnp.int32) + has_north.astype(jnp.int32)
-
-    barrier = pltpu.get_barrier_semaphore()
-
-    def greet(d):
-        pl.semaphore_signal(barrier, inc=1, device_id=target(d), device_id_type=MESH)
-
-    by_side(greet, (4, 6, 2))
-
-    @pl.when(jnp.logical_not(is_last))
-    def _():
-        by_side(greet, (0, 1))
-        pl.when(jnp.logical_not(is_before_last))(lambda: by_side(greet, (5, 7, 3)))
-
     loads = [
         pltpu.make_async_copy(src, dst, local_sem.at[n])
         for n, (src, dst) in enumerate(
@@ -120,7 +103,26 @@
              (cidx_hbm, cidx), (qidx_hbm, qidx), (rband_hbm, rband))
         )
     ]
-    for load in loads:
+    loads[0].start()
+
+    is_first = lon == 0
+    is_last = lon == nlon - 1
+    is_before_last = lon == nlon - 2
+    greeted = 1 + has_south.astype(jnp.int32) + has_north.astype(jnp.int32)
+
+    barrier = pltpu.get_barrier_semaphore()
+
+    def greet(d):
+        pl.semaphore_signal(barrier, inc=1, device_id=target(d), device_id_type=MESH)
+
+    by_side(greet, (4, 6, 2))
+
+    @pl.when(jnp.logical_not(is_last))
+    def _():
+        by_side(greet, (0, 1))
+        pl.when(jnp.logical_not(is_before_last))(lambda: by_side(greet, (5, 7, 3)))
+
+    for load in loads[1:]:
         load.start()
 
     def remote(src, dst, step, n, d):
@@ -272,6 +274,7 @@
     def without_edges(r):
         return jnp.concatenate([r[72:76], r[72:76], r, r[4:8], r[4:8]], axis=0)
 
+    near = jnp.where(lat < nlat // 2, 0, 1)
     for step in range(STEPS):
         if step == 0:
             for d in (2, 3):
@@ -303,33 +306,48 @@
                     ext.append(without_edges(r))
             put_windows(5 + 5 * p, ext)
 
-        wait_recv(step, (0, 1) + ((4, 6) if step == 0 else ()))
-        for side, p in enumerate((3, 0)):
+        def put_halo_windows(i):
             ext = []
             for k in range(3):
-                r = halo[step, side, k].astype(F32)
+                r = halo[step, i, k].astype(F32)
                 if step == 0:
-                    w, x = (edge_in[2 + s, p, k].astype(F32) for s in range(2))
+                    w, x = (edge_in[2 + s, 3 - 3 * i, k].astype(F32) for s in range(2))
                     ext.append(with_edges(r, w, x))
                 else:
                     ext.append(without_edges(r))
-            put_windows(25 * side, ext)
-
-        for i in range(2):
+            for k, block in enumerate(windows(*ext, TILES)):
+                win[25 * i + k] = block.astype(BF16)
+
+        def put_new_states(i):
+            band = rband[i]
+            rows = pl.ds(pl.multiple_of(ROWS * i, ROWS), ROWS)
             for b in range(8):
-                x = win[10 * i + qidx[bands[i], b]]
-                w = drive[bands[i], 128 * b:128 * (b + 1)]
+                x = win[10 * i + qidx[band, b]]
+                w = drive[band, 128 * b:128 * (b + 1)]
                 new = jnp.tanh(pre[i, b] + dot_nt(x, w))
-                states[b, ROWS * i:ROWS * (i + 1)] = new.astype(BF16)
+                states[b, rows] = new.astype(BF16)
                 if step == STEPS - 1:
                     for j in range(16):
                         at = row_of(j, 0)
                         state_out[i, j, :, 128 * b:128 * (b + 1)] = new[at:at + 4].astype(BF16)
+
         if step == 0:
+            wait_recv(step, (0, 1, 4, 6))
+            for i in range(2):
+                put_halo_windows(i)
+            for i in range(2):
+                put_new_states(i)
             loads[5].wait()
+        else:
+            for n in range(2):
+                i = near if n == 0 else 1 - near
+                pl.when((i == 0) & has_south)(message(step, 1).wait_recv)
+                pl.when((i == 1) & has_north)(message(step, 0).wait_recv)
+                put_halo_windows(i)
+                put_new_states(i)
         x = jnp.concatenate([states[c] for c in range(8)], axis=1)
         if step < STEPS - 1:
-            first = jnp.where(lat < nlat // 2, 1, 0)
+            first = 1 - near
             for n in range(2):
                 h = first if n == 0 else 1 - first
                 y = dot_nt(x, read[0, pl.ds(pl.multiple_of(320 * h, 320), 320)])

time: 29.6 us -> 29.1 us (0.983)
  Pallas kernels: 28.8 us -> 28.4 us
    pallas_call x1, Pallas kernels: 28.1 us -> 27.6 us  [per_device(): pl.pallas_call(kernel, out_shape=(pltpu.VMEM(field_state.shape, BF16), pl...]
where the time goes in v6:
time: 29.1 us; the launch traced here: 29 us
  Pallas kernels  28.4 us (98%)
  between operations  0.64 us (2%)
    pallas_call x1, Pallas kernels, per_device(): pl.pallas_call(kernel, out_shape=(pltpu.VMEM(field_state.shape, BF16), pl...  27.6 us
    pallas_call x1, Pallas kernels, per_device(): pl.pallas_call(deliver, out_shape=(jax.ShapeDtypeStruct(field_state.shape...  0.78 us

profile of v6, /device:TPU:8, one launch (start us, length us, event | category | flops | bytes accessed | tf_op | source)
XLA Modules:
  0.0 29.0 jit_solution(10029496489806158067)
XLA Ops:
  0.6 27.6 %forecast.1 = (bf16[4,8,2560]{2,1,0:T(8,128)(2,1)S(1)}, bf16[2,16,4,1024]{3,2,1,0:T(4,128)(2,1)S(1)}) custom-call(s32[2,2,8]{2,1,0:T(2,128)} %bitcast.1, s32[2,8]{1,0:T(2,128)} %qidx_hbm.1, s32[2]{0:T(128)} %rband_hbm.1, bf16[4,8,2560]{2,1,0:T(8,128)(2,1)} %field_hbm.1, bf16[2,16,4,1024]{3,2,1,0:T(4,128)(2,1)} %state_hbm.1, bf16[2,2048,128]{2,1,0:T(8,128)(2,1)} %coup_hbm.1, ...), custom_call_target="tpu_custom_call" | custom-call | tf_op jit(solution)/shard_map/forecast/pallas_call | solution.py:411
  28.2 0.8 %deliver.1 = (bf16[4,8,2560]{2,1,0:T(8,128)(2,1)}, bf16[2,16,4,1024]{3,2,1,0:T(4,128)(2,1)}) custom-call(bf16[4,8,2560]{2,1,0:T(8,128)(2,1)S(1)} %get-tuple-element.4.field_ref, bf16[2,16,4,1024]{3,2,1,0:T(4,128)(2,1)S(1)} %get-tuple-element.5.state_ref), custom_call_target="tpu_custom_call" | custom-call | tf_op jit(solution)/shard_map/deliver/pallas_call | solution.py:458

commit v7 on v6

--- a/solution.py
+++ b/solution.py
@@ -261,15 +261,24 @@
         for k, block in enumerate(windows(*ext, TILES)):
             win[at + k] = block.astype(BF16)
 
-    def with_edges(r, w, x):
+    def western(r, w):
         return jnp.concatenate(
-            [
-                w[0:4], r[72:76], w[4:8], r[4:8], w[8:12], r[12:16],
-                r[16:64],
-                r[64:68], x[0:4], r[72:76], x[4:8], r[4:8], x[8:12],
-            ],
-            axis=0,
+            [w[0:4], r[72:76], w[4:8], r[4:8], w[8:12], r[12:16], r[16:40]], axis=0
         )
+
+    def eastern(r, x):
+        return jnp.concatenate(
+            [r[24:64], r[64:68], x[0:4], r[72:76], x[4:8], r[4:8], x[8:12]], axis=0
+        )
+
+    starts = [(5 + 5 * p, raw.at[0, p], 0, p) for p in range(4)]
+    starts += [(0, halo.at[0, 0], 2, 3), (25, halo.at[0, 1], 2, 0)]
+
+    def put_start_windows(pairs, side, tiles, at, rows):
+        for to, ref, edges, p in pairs:
+            ext = [tiles(ref[k].astype(F32), edge_in[edges + side, p, k].astype(F32)) for k in range(3)]
+            for k, block in enumerate(windows(*ext, rows // 8)):
+                win[to + k, at:at + rows] = block.astype(BF16)
 
     def without_edges(r):
         return jnp.concatenate([r[72:76], r[72:76], r, r[4:8], r[4:8]], axis=0)
@@ -277,11 +286,16 @@
     near = jnp.where(lat < nlat // 2, 0, 1)
     for step in range(STEPS):
         if step == 0:
-            for d in (2, 3):
-                state_message(d).wait_recv()
+            state_message(2).wait_recv()
             for i in range(2):
-                for t in (0, 8):
-                    put_state(i, t)
+                put_state(i, 8)
+            wait_recv(step, (2,))
+            put_start_windows(starts[:4], 1, eastern, 32, 48)
+            wait_recv(step, (0, 1, 4, 6))
+            put_start_windows(starts[4:], 1, eastern, 32, 48)
+            state_message(3).wait_recv()
+            for i in range(2):
+                put_state(i, 0)
         for i in range(2):
             for b in range(8):
                 x = jnp.concatenate(
@@ -293,30 +307,13 @@
                 pre[i, b] = dot_nt(x, w)
         if step == 0:
             wait_recv(step, (3, 5, 7))
-            pl.when(is_first)(send_west)
-            wait_recv(step, (2,))
-        for p in range(4):
-            ext = []
-            for k in range(3):
-                r = raw[step, p, k].astype(F32)
-                if step == 0:
-                    w, x = (edge_in[side, p, k].astype(F32) for side in range(2))
-                    ext.append(with_edges(r, w, x))
-                else:
-                    ext.append(without_edges(r))
-            put_windows(5 + 5 * p, ext)
+            put_start_windows(starts, 0, western, 0, 32)
+        else:
+            for p in range(4):
+                put_windows(5 + 5 * p, [without_edges(raw[step, p, k].astype(F32)) for k in range(3)])
 
         def put_halo_windows(i):
-            ext = []
-            for k in range(3):
-                r = halo[step, i, k].astype(F32)
-                if step == 0:
-                    w, x = (edge_in[2 + s, 3 - 3 * i, k].astype(F32) for s in range(2))
-                    ext.append(with_edges(r, w, x))
-                else:
-                    ext.append(without_edges(r))
-            for k, block in enumerate(windows(*ext, TILES)):
-                win[25 * i + k] = block.astype(BF16)
+            put_windows(25 * i, [without_edges(halo[step, i, k].astype(F32)) for k in range(3)])
 
         def put_new_states(i):
             band = rband[i]
@@ -332,9 +329,6 @@
                         state_out[i, j, :, 128 * b:128 * (b + 1)] = new[at:at + 4].astype(BF16)
 
         if step == 0:
-            wait_recv(step, (0, 1, 4, 6))
-            for i in range(2):
-                put_halo_windows(i)
             for i in range(2):
                 put_new_states(i)
             loads[5].wait()
@@ -359,6 +353,8 @@
                     )
                 pl.when((h == 0) & has_south)(message(step + 1, 0).start)
                 pl.when((h == 1) & has_north)(message(step + 1, 1).start)
+            if step == 0:
+                pl.when(is_first)(send_west)
         else:
             for dy in range(4):
                 y = dot_nt(x, read[0, 160 * dy:160 * dy + 160])

time: 29.1 us -> 28.9 us (level)
  Pallas kernels: 28.4 us -> 28.1 us
where the time goes in v7:
time: 28.9 us; the launch traced here: 28.7 us
  Pallas kernels  28.1 us (97%)
  between operations  0.64 us (2%)
    pallas_call x1, Pallas kernels, per_device(): pl.pallas_call(kernel, out_shape=(pltpu.VMEM(field_state.shape, BF16), pl...  27.3 us
    pallas_call x1, Pallas kernels, per_device(): pl.pallas_call(deliver, out_shape=(jax.ShapeDtypeStruct(field_state.shape...  0.78 us

profile of v7, /device:TPU:8, one launch (start us, length us, event | category | flops | bytes accessed | tf_op | source)
XLA Modules:
  0.0 28.7 jit_solution(17205166647481778065)
XLA Ops:
  0.6 27.3 %forecast.1 = (bf16[4,8,2560]{2,1,0:T(8,128)(2,1)S(1)}, bf16[2,16,4,1024]{3,2,1,0:T(4,128)(2,1)S(1)}) custom-call(s32[2,2,8]{2,1,0:T(2,128)} %bitcast.1, s32[2,8]{1,0:T(2,128)} %qidx_hbm.1, s32[2]{0:T(128)} %rband_hbm.1, bf16[4,8,2560]{2,1,0:T(8,128)(2,1)} %field_hbm.1, bf16[2,16,4,1024]{3,2,1,0:T(4,128)(2,1)} %state_hbm.1, bf16[2,2048,128]{2,1,0:T(8,128)(2,1)} %coup_hbm.1, ...), custom_call_target="tpu_custom_call" | custom-call | tf_op jit(solution)/shard_map/forecast/pallas_call | solution.py:407
  28.0 0.8 %deliver.1 = (bf16[4,8,2560]{2,1,0:T(8,128)(2,1)}, bf16[2,16,4,1024]{3,2,1,0:T(4,128)(2,1)}) custom-call(bf16[4,8,2560]{2,1,0:T(8,128)(2,1)S(1)} %get-tuple-element.4.field_ref, bf16[2,16,4,1024]{3,2,1,0:T(4,128)(2,1)S(1)} %get-tuple-element.5.state_ref), custom_call_target="tpu_custom_call" | custom-call | tf_op jit(solution)/shard_map/deliver/pallas_call | solution.py:454

commit v8 on v7

--- a/solution.py
+++ b/solution.py
@@ -24,6 +24,10 @@
 def row_of(column, member):
     at = column + 2
     return at % TILES * 8 + at // TILES * 4 + member
+
+
+def dot_nn(x, w):
+    return lax.dot_general(x, w, (((1,), (0,)), ((), ())), preferred_element_type=F32)
 
 
 def lanes(rows):
@@ -72,7 +76,7 @@
     field_hbm, state_hbm, coup_hbm, drive_hbm, read_hbm,
     field_out, state_out,
     cidx, qidx, rband,
-    field_in, state_in, coup, drive, read,
+    field_in, state_in, coup, drive, read, drive_t, read_t,
     states, pre, win, raw, halo, edge, edge_in, state_edge, ta, tb, ea, eb,
     local_sem, send_sem, recv_sem, ready,
 ):
@@ -253,9 +257,18 @@
     for i in range(2):
         for t in (2, 4, 6):
             put_state(i, t)
-    for load in loads[3:5] + loads[6:]:
+    for load in loads[3:]:
         load.wait()
     bands = [rband[i] for i in range(2)]
+
+    for band in range(2):
+        for b in range(8):
+            drive_t[band, 128 * b:128 * (b + 1)] = drive[band, 128 * b:128 * (b + 1)].T
+    for h in range(2):
+        for c in range(8):
+            part = read[0, 320 * h:320 * h + 320, 128 * c:128 * (c + 1)]
+            part = jnp.concatenate([part, jnp.zeros((64, 128), BF16)], axis=0)
+            read_t[h, 128 * c:128 * (c + 1)] = part.T
 
     def put_windows(at, ext):
         for k, block in enumerate(windows(*ext, TILES)):
@@ -320,8 +333,8 @@
             rows = pl.ds(pl.multiple_of(ROWS * i, ROWS), ROWS)
             for b in range(8):
                 x = win[10 * i + qidx[band, b]]
-                w = drive[band, 128 * b:128 * (b + 1)]
-                new = jnp.tanh(pre[i, b] + dot_nt(x, w))
+                w = drive_t[band, 128 * b:128 * (b + 1)]
+                new = jnp.tanh(pre[i, b] + dot_nn(x, w))
                 states[b, rows] = new.astype(BF16)
                 if step == STEPS - 1:
                     for j in range(16):
@@ -331,7 +344,6 @@
         if step == 0:
             for i in range(2):
                 put_new_states(i)
-            loads[5].wait()
         else:
             for n in range(2):
                 i = near if n == 0 else 1 - near
@@ -344,8 +356,7 @@
             first = 1 - near
             for n in range(2):
                 h = first if n == 0 else 1 - first
-                y = dot_nt(x, read[0, pl.ds(pl.multiple_of(320 * h, 320), 320)])
-                y = jnp.concatenate([y, jnp.zeros((2 * ROWS, 64), F32)], axis=1)
+                y = dot_nn(x, read_t[h])
                 for i in range(2):
                     put_raw(
                         step + 1, 2 * i + h,
@@ -356,12 +367,17 @@
             if step == 0:
                 pl.when(is_first)(send_west)
         else:
-            for dy in range(4):
-                y = dot_nt(x, read[0, 160 * dy:160 * dy + 160])
+            lane = lanes(ROWS)
+            for h in range(2):
+                y = dot_nn(x, read_t[h])
                 for i in range(2):
-                    at = ROWS * (4 * i + dy)
-                    ta[at:at + ROWS] = y[ROWS * i:ROWS * (i + 1), 0:128]
-                    tb[at:at + ROWS, 0:32] = y[ROWS * i:ROWS * (i + 1), 128:160]
+                    y0, y1, y2 = (y[ROWS * i:ROWS * (i + 1), 128 * k:128 * (k + 1)] for k in range(3))
+                    at = ROWS * (4 * i + 2 * h)
+                    ta[at:at + ROWS] = y0
+                    tb[at:at + ROWS] = y1
+                    r1, r2 = roll(y1, 96), roll(y2, 96)
+                    ta[at + ROWS:at + 2 * ROWS] = jnp.where(lane < 96, r1, r2)
+                    tb[at + ROWS:at + 2 * ROWS] = r2
 
     for m in range(4):
         cols = []
@@ -421,6 +437,8 @@
             pltpu.VMEM(coupling_blocks.shape, BF16),
             pltpu.VMEM(input_blocks.shape, BF16),
             pltpu.VMEM(readout.shape, BF16),
+            pltpu.VMEM(input_blocks.shape, BF16),
+            pltpu.VMEM((2, 1024, 384), BF16),
             pltpu.VMEM((8, 2 * ROWS, 128), BF16),
             pltpu.VMEM((2, 8, ROWS, 128), F32),
             pltpu.VMEM((30, ROWS, 128), BF16),

time: 28.9 us -> 28.4 us (0.983)
  Pallas kernels: 28.1 us -> 27.6 us
    pallas_call x1, Pallas kernels: 27.3 us -> 26.9 us  [per_device(): pl.pallas_call(kernel, out_shape=(pltpu.VMEM(field_state.shape, BF16), pl...]
where the time goes in v8:
time: 28.4 us; the launch traced here: 28.3 us
  Pallas kernels  27.6 us (97%)
  between operations  0.64 us (2%)
    pallas_call x1, Pallas kernels, per_device(): pl.pallas_call(kernel, out_shape=(pltpu.VMEM(field_state.shape, BF16), pl...  26.9 us
    pallas_call x1, Pallas kernels, per_device(): pl.pallas_call(deliver, out_shape=(jax.ShapeDtypeStruct(field_state.shape...  0.78 us

profile of v8, /device:TPU:8, one launch (start us, length us, event | category | flops | bytes accessed | tf_op | source)
XLA Modules:
  0.0 28.3 jit_solution(15245739319394337458)
XLA Ops:
  0.6 26.9 %forecast.1 = (bf16[4,8,2560]{2,1,0:T(8,128)(2,1)S(1)}, bf16[2,16,4,1024]{3,2,1,0:T(4,128)(2,1)S(1)}) custom-call(s32[2,2,8]{2,1,0:T(2,128)} %bitcast.1, s32[2,8]{1,0:T(2,128)} %qidx_hbm.1, s32[2]{0:T(128)} %rband_hbm.1, bf16[4,8,2560]{2,1,0:T(8,128)(2,1)} %field_hbm.1, bf16[2,16,4,1024]{3,2,1,0:T(4,128)(2,1)} %state_hbm.1, bf16[2,2048,128]{2,1,0:T(8,128)(2,1)} %coup_hbm.1, ...), custom_call_target="tpu_custom_call" | custom-call | tf_op jit(solution)/shard_map/forecast/pallas_call | solution.py:423
  27.5 0.8 %deliver.1 = (bf16[4,8,2560]{2,1,0:T(8,128)(2,1)}, bf16[2,16,4,1024]{3,2,1,0:T(4,128)(2,1)}) custom-call(bf16[4,8,2560]{2,1,0:T(8,128)(2,1)S(1)} %get-tuple-element.4.field_ref, bf16[2,16,4,1024]{3,2,1,0:T(4,128)(2,1)S(1)} %get-tuple-element.5.state_ref), custom_call_target="tpu_custom_call" | custom-call | tf_op jit(solution)/shard_map/deliver/pallas_call | solution.py:472

commit v9 on v8

--- a/solution.py
+++ b/solution.py
@@ -146,6 +146,11 @@
             return remote(edge.at[side], edge_in.at[into], step, d, d)
         pair = 0 if dl < 0 else 3
         return remote(edge.at[side, pair], edge_in.at[2 + into, pair], step, d, d)
+
+    def lat_part(step, d, n):
+        pair, side = (0, 1) if d == 0 else (3, 0)
+        blocks = pl.ds(2 * n, 2 - n)
+        return remote(raw.at[step, pair, blocks], halo.at[step, side, blocks], step, d + 4 * n, d)
 
     def state_message(d):
         side, into = (0, 1) if DIRS[d][1] < 0 else (1, 0)
@@ -345,25 +350,39 @@
             for i in range(2):
                 put_new_states(i)
         else:
-            for n in range(2):
-                i = near if n == 0 else 1 - near
-                pl.when((i == 0) & has_south)(message(step, 1).wait_recv)
-                pl.when((i == 1) & has_north)(message(step, 0).wait_recv)
+            for turn in range(2):
+                i = near if turn == 0 else 1 - near
+                for n in range(2):
+                    pl.when((i == 0) & has_south)(lat_part(step, 1, n).wait_recv)
+                    pl.when((i == 1) & has_north)(lat_part(step, 0, n).wait_recv)
                 put_halo_windows(i)
                 put_new_states(i)
         x = jnp.concatenate([states[c] for c in range(8)], axis=1)
         if step < STEPS - 1:
-            first = 1 - near
-            for n in range(2):
-                h = first if n == 0 else 1 - first
-                y = dot_nn(x, read_t[h])
-                for i in range(2):
-                    put_raw(
-                        step + 1, 2 * i + h,
-                        tuple(y[ROWS * i:ROWS * (i + 1), 128 * k:128 * (k + 1)] for k in range(3)),
-                    )
-                pl.when((h == 0) & has_south)(message(step + 1, 0).start)
-                pl.when((h == 1) & has_north)(message(step + 1, 1).start)
+            far = 1 - near
+
+            def put(i, h, y, first=0):
+                for k in range(y.shape[1] // 128):
+                    raw[step + 1, 2 * i + h, first + k] = y[:, 128 * k:128 * (k + 1)].astype(BF16)
+
+            def go(h, parts):
+                for n in parts:
+                    pl.when((h == 0) & has_south)(lat_part(step + 1, 0, n).start)
+                    pl.when((h == 1) & has_north)(lat_part(step + 1, 1, n).start)
+
+            far_rows = pl.ds(pl.multiple_of(ROWS * far, ROWS), ROWS)
+            x_far = jnp.concatenate([states[c, far_rows] for c in range(8)], axis=1)
+            put(far, far, dot_nn(x_far, read_t[far, :, 0:256]))
+            go(far, (0,))
+            put(far, far, dot_nn(x_far, read_t[far, :, 256:384]), 2)
+            go(far, (1,))
+            y = dot_nn(x, read_t[near])
+            for i in range(2):
+                put(i, near, y[ROWS * i:ROWS * (i + 1)])
+            go(near, (0, 1))
+            near_rows = pl.ds(pl.multiple_of(ROWS * near, ROWS), ROWS)
+            x_near = jnp.concatenate([states[c, near_rows] for c in range(8)], axis=1)
+            put(near, far, dot_nn(x_near, read_t[far]))
             if step == 0:
                 pl.when(is_first)(send_west)
         else:
@@ -403,7 +422,8 @@
     for d in (2, 3):
         state_message(d).wait_send()
     for step in range(1, STEPS):
-        by_side(lambda d: message(step, d).wait_send(), (0, 1))
+        for n in range(2):
+            by_side(lambda d: lat_part(step, d, n).wait_send(), (0, 1))
 
 
 def deliver(field_ref, state_ref, field_out, state_out, sems):
@@ -447,10 +467,10 @@
             pltpu.VMEM((2, 4, 3, 16, 128), BF16),
             pltpu.VMEM((4, 4, 3, 16, 128), BF16),
             pltpu.VMEM((2, 2, 2, 4, 1024), BF16),
-            pltpu.VMEM((8 * ROWS, 128), F32),
-            pltpu.VMEM((8 * ROWS, 128), F32),
-            pltpu.VMEM((2, 128, 128), F32),
-            pltpu.VMEM((2, 128, 128), F32),
+            pltpu.VMEM((9 * ROWS, 128), F32),
+            pltpu.VMEM((9 * ROWS, 128), F32),
+            pltpu.VMEM((2, 144, 128), F32),
+            pltpu.VMEM((2, 144, 128), F32),
             pltpu.SemaphoreType.DMA((9,)),
             pltpu.SemaphoreType.DMA((STEPS, 10)),
             pltpu.SemaphoreType.DMA((STEPS, 10)),

time: 28.4 us -> 28.3 us (level)
  no operation moved by 1% of the time
where the time goes in v9:
time: 28.3 us; the launch traced here: 28.2 us
  Pallas kernels  27.5 us (97%)
  between operations  0.64 us (2%)
    pallas_call x1, Pallas kernels, per_device(): pl.pallas_call(kernel, out_shape=(pltpu.VMEM(field_state.shape, BF16), pl...  26.8 us
    pallas_call x1, Pallas kernels, per_device(): pl.pallas_call(deliver, out_shape=(jax.ShapeDtypeStruct(field_state.shape...  0.78 us

profile of v9, /device:TPU:8, one launch (start us, length us, event | category | flops | bytes accessed | tf_op | source)
XLA Modules:
  0.0 28.2 jit_solution(10720447465638062704)
XLA Ops:
  0.6 26.8 %forecast.1 = (bf16[4,8,2560]{2,1,0:T(8,128)(2,1)S(1)}, bf16[2,16,4,1024]{3,2,1,0:T(4,128)(2,1)S(1)}) custom-call(s32[2,2,8]{2,1,0:T(2,128)} %bitcast.1, s32[2,8]{1,0:T(2,128)} %qidx_hbm.1, s32[2]{0:T(128)} %rband_hbm.1, bf16[4,8,2560]{2,1,0:T(8,128)(2,1)} %field_hbm.1, bf16[2,16,4,1024]{3,2,1,0:T(4,128)(2,1)} %state_hbm.1, bf16[2,2048,128]{2,1,0:T(8,128)(2,1)} %coup_hbm.1, ...), custom_call_target="tpu_custom_call" | custom-call | tf_op jit(solution)/shard_map/forecast/pallas_call | solution.py:443
  27.4 0.8 %deliver.1 = (bf16[4,8,2560]{2,1,0:T(8,128)(2,1)}, bf16[2,16,4,1024]{3,2,1,0:T(4,128)(2,1)}) custom-call(bf16[4,8,2560]{2,1,0:T(8,128)(2,1)S(1)} %get-tuple-element.4.field_ref, bf16[2,16,4,1024]{3,2,1,0:T(4,128)(2,1)S(1)} %get-tuple-element.5.state_ref), custom_call_target="tpu_custom_call" | custom-call | tf_op jit(solution)/shard_map/deliver/pallas_call | solution.py:492

commit v10 on v9

--- a/solution.py
+++ b/solution.py
@@ -76,7 +76,7 @@
     field_hbm, state_hbm, coup_hbm, drive_hbm, read_hbm,
     field_out, state_out,
     cidx, qidx, rband,
-    field_in, state_in, coup, drive, read, drive_t, read_t,
+    field_in, state_in, coup, drive, read, coup_t, drive_t, read_t,
     states, pre, win, raw, halo, edge, edge_in, state_edge, ta, tb, ea, eb,
     local_sem, send_sem, recv_sem, ready,
 ):
@@ -267,6 +267,8 @@
     bands = [rband[i] for i in range(2)]
 
     for band in range(2):
+        for b in range(16):
+            coup_t[band, 128 * b:128 * (b + 1)] = coup[band, 128 * b:128 * (b + 1)].T
         for b in range(8):
             drive_t[band, 128 * b:128 * (b + 1)] = drive[band, 128 * b:128 * (b + 1)].T
     for h in range(2):
@@ -319,10 +321,7 @@
                 x = jnp.concatenate(
                     [states[cidx[bands[i], k, b], ROWS * i:ROWS * (i + 1)] for k in range(2)], axis=1
                 )
-                w = jnp.concatenate(
-                    [coup[bands[i], (2 * b + k) * 128:(2 * b + k + 1) * 128] for k in range(2)], axis=1
-                )
-                pre[i, b] = dot_nt(x, w)
+                pre[i, b] = dot_nn(x, coup_t[bands[i], 256 * b:256 * (b + 1)])
         if step == 0:
             wait_recv(step, (3, 5, 7))
             put_start_windows(starts, 0, western, 0, 32)
@@ -457,6 +456,7 @@
             pltpu.VMEM(coupling_blocks.shape, BF16),
             pltpu.VMEM(input_blocks.shape, BF16),
             pltpu.VMEM(readout.shape, BF16),
+            pltpu.VMEM(coupling_blocks.shape, BF16),
             pltpu.VMEM(input_blocks.shape, BF16),
             pltpu.VMEM((2, 1024, 384), BF16),
             pltpu.VMEM((8, 2 * ROWS, 128), BF16),

time: 28.3 us -> 28.3 us (level)
  no operation moved by 1% of the time
where the time goes in v10:
time: 28.3 us; the launch traced here: 28.2 us
  Pallas kernels  27.5 us (97%)
  between operations  0.64 us (2%)
    pallas_call x1, Pallas kernels, per_device(): pl.pallas_call(kernel, out_shape=(pltpu.VMEM(field_state.shape, BF16), pl...  26.8 us
    pallas_call x1, Pallas kernels, per_device(): pl.pallas_call(deliver, out_shape=(jax.ShapeDtypeStruct(field_state.shape...  0.78 us

profile of v10, /device:TPU:8, one launch (start us, length us, event | category | flops | bytes accessed | tf_op | source)
XLA Modules:
  0.0 28.2 jit_solution(326858215247106669)
XLA Ops:
  0.6 26.8 %forecast.1 = (bf16[4,8,2560]{2,1,0:T(8,128)(2,1)S(1)}, bf16[2,16,4,1024]{3,2,1,0:T(4,128)(2,1)S(1)}) custom-call(s32[2,2,8]{2,1,0:T(2,128)} %bitcast.1, s32[2,8]{1,0:T(2,128)} %qidx_hbm.1, s32[2]{0:T(128)} %rband_hbm.1, bf16[4,8,2560]{2,1,0:T(8,128)(2,1)} %field_hbm.1, bf16[2,16,4,1024]{3,2,1,0:T(4,128)(2,1)} %state_hbm.1, bf16[2,2048,128]{2,1,0:T(8,128)(2,1)} %coup_hbm.1, ...), custom_call_target="tpu_custom_call" | custom-call | tf_op jit(solution)/shard_map/forecast/pallas_call | solution.py:442
  27.4 0.8 %deliver.1 = (bf16[4,8,2560]{2,1,0:T(8,128)(2,1)}, bf16[2,16,4,1024]{3,2,1,0:T(4,128)(2,1)}) custom-call(bf16[4,8,2560]{2,1,0:T(8,128)(2,1)S(1)} %get-tuple-element.4.field_ref, bf16[2,16,4,1024]{3,2,1,0:T(4,128)(2,1)S(1)} %get-tuple-element.5.state_ref), custom_call_target="tpu_custom_call" | custom-call | tf_op jit(solution)/shard_map/deliver/pallas_call | solution.py:492
